TPU v7x, 256 devices: a whole 4x4x8 slice. The times are simulated.
256 devices in a mesh: dp: 32 (over x, y, z_lo), ctx: 8 (over z_hi, core).
Axes of the slice: x: 4, y: 4, z: 8 (z_hi: 4, z_lo: 2; z = z_hi * 2 + z_lo), core: 2. Of those that a mesh axis runs over, the one named last changes fastest.
Arguments:
- queries: bfloat16 [32, 1024, 4096], P('dp', 'ctx'), may hold values from -80 to 80
- keys: bfloat16 [32, 1024, 512], P('dp', 'ctx'), may hold values from -80 to 80
- values: bfloat16 [32, 1024, 512], P('dp', 'ctx'), may hold values from -6 to 6
- q_gain: float32 [128], replicated, may hold values from 0.8 to 2
- k_gain: float32 [128], replicated, may hold values from 0.8 to 2
- out_grad: bfloat16 [32, 1024, 4096], P('dp', 'ctx'), may hold values from -18 to 18
- block_order: int32 [32, 8], P('dp'), may hold values from 0 to 7, each once within a row
Outputs:
- grad_queries: bfloat16 [32, 1024, 4096], P('dp', 'ctx')
- grad_keys: bfloat16 [32, 1024, 512], P('dp', 'ctx')
- grad_values: bfloat16 [32, 1024, 512], P('dp', 'ctx')
- grad_q_gain: float32 [128], replicated
- grad_k_gain: float32 [128], replicated
Inputs may be any that keep to these rules, and one draw needn't show every extreme that they name: `block_order`: each row lists every block index once.
All inputs are finite; a program needn't handle non-finite values.
Results may differ from a plain program's by a relative error of at most 0.03.
Values may be sent and summed in bfloat16 or wider, within the bound.
A program may use at most 128 MiB of HBM per device.

v0:
```python
import math

import jax
import jax.numpy as jnp
from jax import lax
from jax.experimental import pallas as pl
from jax.experimental.pallas import tpu as pltpu
from jax.sharding import PartitionSpec as P

HQ = 32
HK = 4
HD = 128
T = 128
EPS = 1e-06
SCALE = 1.0 / math.sqrt(HD)
EXP2_SCALE = SCALE * math.log2(math.e)
NEG = -1e30
BF = jnp.bfloat16
F32 = jnp.float32
MESH = pl.DeviceIdType.MESH
NT = (((1,), (1,)), ((), ()))
NN = (((1,), (0,)), ((), ()))

STEP_FORWARD = 3
STEP_REDUCE = 11
STEP_FINISH = 15


def dot(a, b, dims):
    return lax.dot_general(a, b, dims, preferred_element_type=F32)


def make_bias(bias, order, chip, core):
    keys_at = lax.broadcasted_iota(jnp.int32, (T, T), 0)
    rows_at = lax.broadcasted_iota(jnp.int32, (T, T), 1)
    for rel in range(2):
        mine = 2 * chip + (core if rel == 0 else 1 - core)
        own = order[0, mine]
        for j in range(8):
            key_pos = order[0, j] * T + keys_at
            row_pos = own * T + rows_at
            bias[rel, j] = jnp.where(key_pos <= row_pos, 0.0, NEG)


def chunk(u, rel, hp, q_buf, g_buf, kv, kt, bias, q_gain, acc, dq_buf, gain_acc, e_scr, d_scr, p_scr, ds_scr):
    cols = pl.ds(pl.multiple_of(hp * 256, 256), 256)
    q2 = q_buf[u, rel, :, cols]
    g2 = g_buf[u, rel, :, cols]
    q = jnp.concatenate([q2[:, :HD], q2[:, HD:]], 0).astype(F32)
    g = jnp.concatenate([g2[:, :HD], g2[:, HD:]], 0)
    factor = lax.rsqrt(jnp.mean(q * q, -1, keepdims=True) + EPS)
    q_unit = q * factor
    gain = q_gain[...]
    qn = (q_unit * gain).astype(BF)
    e_scr[...] = dot(kv[u, 0].reshape(8 * T, HD), qn, NT)
    d_scr[...] = dot(kv[u, 1].reshape(8 * T, HD), g, NT)
    total = jnp.zeros((8, 256), F32)
    cross = jnp.zeros((8, 256), F32)
    half = 64
    for b in range(8 * T // half):
        at = pl.ds(b * half, half)
        j, off = divmod(b * half, T)
        tile = bias[rel, j, off : off + half, :]
        tile = jnp.concatenate([tile, tile], 1)
        e = jnp.exp2(e_scr[at, :] * EXP2_SCALE + tile)
        e_scr[at, :] = e
        total = total + jnp.sum(e.reshape(half // 8, 8, 256), 0)
        cross = cross + jnp.sum((e * d_scr[at, :]).reshape(half // 8, 8, 256), 0)
    inv = 1.0 / jnp.sum(total, 0, keepdims=True)
    row_dots = jnp.sum(cross, 0, keepdims=True) * inv
    for b in range(8 * T // half):
        at = pl.ds(b * half, half)
        p = e_scr[at, :] * inv
        p_scr[at, :] = p.astype(BF)
        ds_scr[at, :] = (p * (d_scr[at, :] - row_dots)).astype(BF)
    acc[u, 1] += dot(p_scr[...], g, NN)
    acc[u, 0] += dot(ds_scr[...], qn, NN)
    dq = dot(kt[...], ds_scr[...], NN).T * SCALE
    gain_acc[0] += jnp.sum((dq * q_unit).reshape(32, 8, HD), 0)
    scaled = dq * gain
    mean = jnp.mean(scaled * q_unit, -1, keepdims=True)
    out = (factor * (scaled - q_unit * mean)).astype(BF)
    dq_buf[u, rel, :, cols] = jnp.concatenate([out[:T], out[T:]], 1)


def kernel(
    order,
    q_hbm,
    k_hbm,
    v_hbm,
    q_gain,
    k_gain,
    g_hbm,
    dq_hbm,
    dk_hbm,
    dv_hbm,
    q_gain_out,
    k_gain_out,
    k_in,
    v_in,
    q_buf,
    g_buf,
    own_kv,
    kv,
    kt,
    bias,
    acc,
    dq_buf,
    gain_acc,
    e_scr,
    d_scr,
    p_scr,
    ds_scr,
    b1_out,
    b1_in,
    b2_out,
    b2_in,
    sib_out,
    sib_in,
    dk_buf,
    dv_buf,
    g1_in,
    g2_in,
    g3_in,
    load_sem,
    qx_send,
    qx_recv,
    s1_send,
    s1_recv,
    s2_send,
    s2_recv,
    sk_send,
    sk_recv,
    b1_send,
    b1_recv,
    b2_send,
    b2_recv,
    sb_send,
    sb_recv,
    out_sem,
    ox_send,
    ox_recv,
    g1_send,
    g1_recv,
    g2_send,
    g2_recv,
    g3_send,
    g3_recv,
    fin_sem,
):
    ctx = lax.axis_index("ctx")
    dp = lax.axis_index("dp")
    chip = ctx // 2
    core = ctx % 2
    other = 1 - core
    sibling = 2 * chip + other
    nxt = lax.rem(chip + 1, 4)
    prv = lax.rem(chip + 3, 4)
    opp = lax.rem(chip + 2, 4)
    near = (nxt, prv)
    dp_x = dp // 8
    dp_y = (dp // 2) % 4
    dp_z = dp % 2
    xz = dp_x * 2 + dp_z

    def xz_peer(m):
        return (m // 2) * 8 + dp_y * 2 + m % 2

    def y_peer(m):
        return dp_x * 8 + m * 2 + dp_z

    def remote(src, dst, ssem, rsem, dev):
        return pltpu.make_async_remote_copy(
            src_ref=src, dst_ref=dst, send_sem=ssem, recv_sem=rsem, device_id=dev, device_id_type=MESH
        )

    def head_cols(core_at, u):
        return pl.ds(pl.multiple_of(core_at * 2048 + u * 1024, 1024), 1024)

    load_k = pltpu.make_async_copy(k_hbm.at[0], k_in, load_sem.at[0])
    load_v = pltpu.make_async_copy(v_hbm.at[0], v_in, load_sem.at[1])
    load_k.start()
    load_v.start()
    load_q = []
    for u in range(2):
        pair = (
            pltpu.make_async_copy(q_hbm.at[0, :, head_cols(core, u)], q_buf.at[u, 0], load_sem.at[2 + 2 * u]),
            pltpu.make_async_copy(g_hbm.at[0, :, head_cols(core, u)], g_buf.at[u, 0], load_sem.at[3 + 2 * u]),
        )
        load_q.append(pair)
        for c in pair:
            c.start()

    barrier = pltpu.get_barrier_semaphore()
    for r in range(1, 8):
        pl.semaphore_signal(barrier, inc=1, device_id={"ctx": lax.rem(ctx + r, 8)}, device_id_type=MESH)
        pl.semaphore_signal(barrier, inc=1, device_id={"dp": xz_peer(lax.rem(xz + r, 8))}, device_id_type=MESH)
    for r in range(1, 4):
        pl.semaphore_signal(barrier, inc=1, device_id={"dp": y_peer(lax.rem(dp_y + r, 4))}, device_id_type=MESH)

    load_k.wait()
    load_v.wait()
    k_gain_row = k_gain[...]
    for h in range(HK):
        block = k_in[:, h * HD : (h + 1) * HD].astype(F32)
        factor = lax.rsqrt(jnp.mean(block * block, -1, keepdims=True) + EPS)
        own_kv[h, 0] = (block * factor * k_gain_row).astype(BF)
        own_kv[h, 1] = v_in[:, h * HD : (h + 1) * HD]
    for u in range(2):
        for part in range(2):
            kv[u, part, ctx] = own_kv[2 * core + u, part]
    gain_acc[...] = jnp.zeros_like(gain_acc)
    acc[...] = jnp.zeros_like(acc)

    pl.semaphore_wait(barrier, 17)

    def stage1(u, d, dest_core, part):
        return remote(
            own_kv.at[2 * dest_core + u, part],
            kv.at[u, part, ctx],
            s1_send.at[u, d, dest_core, part],
            s1_recv.at[u, d, core, part],
            {"ctx": 2 * near[d] + dest_core},
        )

    def stage1_arrival(u, d, src_core, part):
        j = 2 * near[1 - d] + src_core
        return remote(
            kv.at[u, part, j], kv.at[u, part, j], s1_send.at[u, d, src_core, part], s1_recv.at[u, d, src_core, part], {"ctx": sibling}
        )

    def sibling_kv(u):
        return remote(own_kv.at[2 * other + u], kv.at[u, :, ctx], sk_send.at[u], sk_recv.at[u], {"ctx": sibling})

    def sibling_kv_arrival(u):
        return remote(own_kv.at[2 * core + u], kv.at[u, :, sibling], sk_send.at[u], sk_recv.at[u], {"ctx": sibling})

    def stage2(u, d, src_core):
        j = 2 * near[1 - d] + src_core
        return remote(
            kv.at[u, d, j], kv.at[u, d, j], s2_send.at[u, d, src_core], s2_recv.at[u, d, src_core], {"ctx": 2 * near[d] + core}
        )

    def stage2_arrival(u, d, src_core):
        j = 2 * opp + src_core
        return remote(
            kv.at[u, d, j], kv.at[u, d, j], s2_send.at[u, d, src_core], s2_recv.at[u, d, src_core], {"ctx": sibling}
        )

    def q_exchange(u):
        return (
            remote(q_hbm.at[0, :, head_cols(other, u)], q_buf.at[u, 1], qx_send.at[u, 0], qx_recv.at[u, 0], {"ctx": sibling}),
            remote(g_hbm.at[0, :, head_cols(other, u)], g_buf.at[u, 1], qx_send.at[u, 1], qx_recv.at[u, 1], {"ctx": sibling}),
        )

    for u in range(2):
        for first in range(2):
            for d in range(2):
                for dest_core in range(2):
                    stage1(u, d, dest_core, d if first == 0 else 1 - d).start()
        sibling_kv(u).start()
        for c in q_exchange(u):
            c.start()

    make_bias(bias, order, chip, core)

    def forward(u):
        for src_core in range(2):
            for d in range(2):
                stage1_arrival(u, d, src_core, d).wait_recv()
                stage2(u, d, src_core).start()

    def finish_gather(u):
        for src_core in range(2):
            for d in range(2):
                stage1_arrival(u, d, src_core, 1 - d).wait_recv()
        sibling_kv_arrival(u).wait_recv()
        for src_core in range(2):
            for d in range(2):
                stage2_arrival(u, d, src_core).wait_recv()
        kt[...] = kv[u, 0].reshape(8 * T, HD).T

    def b1(u, d):
        return remote(b1_out.at[u, d], b1_in.at[u, d], b1_send.at[u, d], b1_recv.at[u, d], {"ctx": 2 * near[d] + core})

    def b2(u, d, dest_core, part):
        return remote(
            b2_out.at[u, d, dest_core, part],
            b2_in.at[u, d, core, part],
            b2_send.at[u, d, dest_core, part],
            b2_recv.at[u, d, core, part],
            {"ctx": 2 * near[d] + dest_core},
        )

    def b2_arrival(u, d, src_core, part):
        return remote(
            b2_out.at[u, d, src_core, part],
            b2_in.at[u, d, src_core, part],
            b2_send.at[u, d, src_core, part],
            b2_recv.at[u, d, src_core, part],
            {"ctx": sibling},
        )

    def sibling_sum(u):
        return remote(sib_out.at[u], sib_in.at[u], sb_send.at[u], sb_recv.at[u], {"ctx": sibling})

    def partial_sum(u, part, j):
        block = acc[u, part, pl.ds(pl.multiple_of(j * T, T), T), :]
        return block * SCALE if part == 0 else block

    def reduce_start(u):
        for d in range(2):
            for dest_core in range(2):
                b1_out[u, d, dest_core] = partial_sum(u, d, 2 * opp + dest_core).astype(BF)
            b1(u, d).start()
        for d in range(2):
            for dest_core in range(2):
                b2_out[u, d, dest_core, 1 - d] = partial_sum(u, 1 - d, 2 * near[d] + dest_core).astype(BF)
                b2(u, d, dest_core, 1 - d).start()
        for part in range(2):
            sib_out[u, part] = partial_sum(u, part, sibling).astype(BF)
        sibling_sum(u).start()
        k_rows = kv[u, 0].reshape(8 * T, HD).astype(F32)
        gain_acc[1] += jnp.sum((acc[u, 0] * k_rows).reshape(T, 8, HD), 0)

    def reduce_middle(u):
        for d in range(2):
            b1(u, d).wait_recv()
            for dest_core in range(2):
                own = partial_sum(u, d, 2 * near[d] + dest_core)
                b2_out[u, d, dest_core, d] = (own + b1_in[u, d, dest_core].astype(F32)).astype(BF)
                b2(u, d, dest_core, d).start()

    def reduce_finish(u):
        sibling_sum(u).wait_recv()
        for d in range(2):
            for src_core in range(2):
                for part in range(2):
                    b2_arrival(u, d, src_core, part).wait_recv()
        for rel in range(2):
            at = core if rel == 0 else other
            sums = []
            for part in range(2):
                own = partial_sum(u, part, ctx) if rel == 0 else sib_in[u, part].astype(F32)
                sums.append(own + b2_in[u, 0, at, part].astype(F32) + b2_in[u, 1, at, part].astype(F32))
            cols = pl.ds(pl.multiple_of(at * 256 + u * HD, HD), HD)
            block = k_in[:, cols].astype(F32)
            factor = lax.rsqrt(jnp.mean(block * block, -1, keepdims=True) + EPS)
            unit = block * factor
            scaled = sums[0] * k_gain_row
            mean = jnp.mean(scaled * unit, -1, keepdims=True)
            dk_buf[:, cols] = (factor * (scaled - unit * mean)).astype(BF)
            dv_buf[:, cols] = sums[1].astype(BF)

    def out_local(u):
        return pltpu.make_async_copy(dq_buf.at[u, 0], dq_hbm.at[0, :, head_cols(core, u)], out_sem.at[u])

    def out_remote(u):
        return remote(dq_buf.at[u, 1], dq_hbm.at[0, :, head_cols(core, u)], ox_send.at[u], ox_recv.at[u], {"ctx": sibling})

    def out_arrival(u):
        return remote(dq_buf.at[u, 1], dq_hbm.at[0, :, head_cols(other, u)], ox_send.at[u], ox_recv.at[u], {"ctx": sibling})

    forward(0)
    finish_gather(0)

    def step(t, carry):
        u = t // 8
        rel = (t % 8) // 4
        hp = t % 4

        @pl.when(t == 0)
        def _():
            for c in load_q[0]:
                c.wait()

        @pl.when(t == STEP_FORWARD)
        def _():
            forward(1)

        @pl.when(t == 4)
        def _():
            out_local(0).start()
            for c in q_exchange(0):
                c.wait_recv()

        @pl.when(t == 8)
        def _():
            out_remote(0).start()
            reduce_start(0)
            finish_gather(1)
            for c in load_q[1]:
                c.wait()

        @pl.when(t == STEP_REDUCE)
        def _():
            reduce_middle(0)

        @pl.when(t == 12)
        def _():
            out_local(1).start()
            for c in q_exchange(1):
                c.wait_recv()

        @pl.when(t == STEP_FINISH)
        def _():
            reduce_finish(0)

        chunk(u, rel, hp, q_buf, g_buf, kv, kt, bias, q_gain, acc, dq_buf, gain_acc, e_scr, d_scr, p_scr, ds_scr)
        return carry

    lax.fori_loop(0, 16, step, 0)
    reduce_start(1)
    out_remote(1).start()

    def g1(r):
        return remote(g1_in.at[ctx], g1_in.at[ctx], g1_send.at[r], g1_recv.at[ctx], {"ctx": lax.rem(ctx + r, 8)})

    def g1_arrival(r):
        j = lax.rem(ctx + r, 8)
        return remote(g1_in.at[j], g1_in.at[j], g1_send.at[r], g1_recv.at[j], {"ctx": sibling})

    def g2(r):
        return remote(g2_in.at[xz], g2_in.at[xz], g2_send.at[r], g2_recv.at[xz], {"dp": xz_peer(lax.rem(xz + r, 8))})

    def g2_arrival(r):
        j = lax.rem(xz + r, 8)
        return remote(g2_in.at[j], g2_in.at[j], g2_send.at[r], g2_recv.at[j], {"ctx": sibling})

    def g3(r):
        return remote(g3_in.at[dp_y], g3_in.at[dp_y], g3_send.at[r], g3_recv.at[dp_y], {"dp": y_peer(lax.rem(dp_y + r, 4))})

    def g3_arrival(r):
        j = lax.rem(dp_y + r, 4)
        return remote(g3_in.at[j], g3_in.at[j], g3_send.at[r], g3_recv.at[j], {"ctx": sibling})

    g1_in[ctx] = gain_acc[...]
    for r in range(1, 8):
        g1(r).start()
    reduce_middle(1)
    for r in range(1, 8):
        g1_arrival(r).wait_recv()
    g2_in[xz] = jnp.sum(g1_in[...], 0)
    for r in range(1, 8):
        g2(r).start()
    for r in range(1, 8):
        g2_arrival(r).wait_recv()
    g3_in[dp_y] = jnp.sum(g2_in[...], 0)
    for r in range(1, 4):
        g3(r).start()
    reduce_finish(1)
    fin_k = pltpu.make_async_copy(dk_buf, dk_hbm.at[0], fin_sem.at[0])
    fin_v = pltpu.make_async_copy(dv_buf, dv_hbm.at[0], fin_sem.at[1])
    fin_k.start()
    fin_v.start()
    for r in range(1, 4):
        g3_arrival(r).wait_recv()
    gains = jnp.sum(jnp.sum(g3_in[...], 0), 1, keepdims=True)
    q_gain_out[...] = gains[0]
    k_gain_out[...] = gains[1] * SCALE / k_gain_row

    for u in range(2):
        for d in range(2):
            for dest_core in range(2):
                for part in range(2):
                    stage1(u, d, dest_core, part).wait_send()
                    b2(u, d, dest_core, part).wait_send()
                stage2(u, d, dest_core).wait_send()
            b1(u, d).wait_send()
        sibling_kv(u).wait_send()
        sibling_sum(u).wait_send()
        for c in q_exchange(u):
            c.wait_send()
        out_local(u).wait()
        out_remote(u).wait_send()
        out_arrival(u).wait_recv()
    for r in range(1, 8):
        g1(r).wait_send()
        g2(r).wait_send()
    for r in range(1, 4):
        g3(r).wait_send()
    fin_k.wait()
    fin_v.wait()


def on_device(queries, keys, values, q_gain, k_gain, out_grad, block_order):
    hbm = pl.BlockSpec(memory_space=pl.ANY)
    vmem = pl.BlockSpec(memory_space=pltpu.VMEM)
    smem = pl.BlockSpec(memory_space=pltpu.SMEM)
    dma = pltpu.SemaphoreType.DMA
    dq, dk, dv, dqg, dkg = pl.pallas_call(
        kernel,
        out_shape=(
            jax.ShapeDtypeStruct(queries.shape, BF),
            jax.ShapeDtypeStruct(keys.shape, BF),
            jax.ShapeDtypeStruct(values.shape, BF),
            jax.ShapeDtypeStruct((1, HD), F32),
            jax.ShapeDtypeStruct((1, HD), F32),
        ),
        in_specs=[smem, hbm, hbm, hbm, vmem, vmem, hbm],
        out_specs=(hbm, hbm, hbm, vmem, vmem),
        scratch_shapes=[
            pltpu.VMEM((T, HK * HD), BF),
            pltpu.VMEM((T, HK * HD), BF),
            pltpu.VMEM((2, 2, T, 1024), BF),
            pltpu.VMEM((2, 2, T, 1024), BF),
            pltpu.VMEM((HK, 2, T, HD), BF),
            pltpu.VMEM((2, 2, 8, T, HD), BF),
            pltpu.VMEM((HD, 8 * T), BF),
            pltpu.VMEM((2, 8, T, T), F32),
            pltpu.VMEM((2, 2, 8 * T, HD), F32),
            pltpu.VMEM((2, 2, T, 1024), BF),
            pltpu.VMEM((2, 8, HD), F32),
            pltpu.VMEM((8 * T, 256), F32),
            pltpu.VMEM((8 * T, 256), F32),
            pltpu.VMEM((8 * T, 256), BF),
            pltpu.VMEM((8 * T, 256), BF),
            pltpu.VMEM((2, 2, 2, T, HD), BF),
            pltpu.VMEM((2, 2, 2, T, HD), BF),
            pltpu.VMEM((2, 2, 2, 2, T, HD), BF),
            pltpu.VMEM((2, 2, 2, 2, T, HD), BF),
            pltpu.VMEM((2, 2, T, HD), BF),
            pltpu.VMEM((2, 2, T, HD), BF),
            pltpu.VMEM((T, HK * HD), BF),
            pltpu.VMEM((T, HK * HD), BF),
            pltpu.VMEM((8, 2, 8, HD), F32),
            pltpu.VMEM((8, 2, 8, HD), F32),
            pltpu.VMEM((4, 2, 8, HD), F32),
            dma((6,)),
            dma((2, 2)),
            dma((2, 2)),
            dma((2, 2, 2, 2)),
            dma((2, 2, 2, 2)),
            dma((2, 2, 2)),
            dma((2, 2, 2)),
            dma((2,)),
            dma((2,)),
            dma((2, 2)),
            dma((2, 2)),
            dma((2, 2, 2, 2)),
            dma((2, 2, 2, 2)),
            dma((2,)),
            dma((2,)),
            dma((2,)),
            dma((2,)),
            dma((2,)),
            dma((8,)),
            dma((8,)),
            dma((8,)),
            dma((8,)),
            dma((4,)),
            dma((4,)),
            dma((2,)),
        ],
        compiler_params=pltpu.CompilerParams(
            collective_id=0, has_side_effects=True, vmem_limit_bytes=40 * 1024 * 1024
        ),
    )(block_order, queries, keys, values, q_gain.reshape(1, HD), k_gain.reshape(1, HD), out_grad)
    return dq, dk, dv, dqg.reshape(HD), dkg.reshape(HD)


def solution(mesh):
    placed = (
        P("dp", "ctx", None),
        P("dp", "ctx", None),
        P("dp", "ctx", None),
        P(),
        P(),
        P("dp", "ctx", None),
        P("dp", None),
    )
    return jax.shard_map(
        on_device,
        mesh=mesh,
        in_specs=placed,
        out_specs=(P("dp", "ctx", None), P("dp", "ctx", None), P("dp", "ctx", None), P(), P()),
        check_vma=False,
    )
```

profile of v0, /device:TPU:1, one launch (start us, length us, event | category | flops | bytes accessed | tf_op | source)
XLA Modules:
  0.0 79.9 jit_solution(1265695974744171195)
XLA Ops:
  0.6 0.0 copy-start.4
  0.6 0.0 copy-start.5
  0.7 0.0 copy-start.6
  0.7 0.6 copy-done.4
  1.3 0.0 copy-done.5
  1.3 0.0 copy-done.6
  1.3 0.0 copy-start
  1.3 1.2 %copy-done = bf16[1,128,4096]{2,1,0:T(8,128)(2,1)S(1)} copy-done((bf16[1,128,4096]{2,1,0:T(8,128)(2,1)S(1)}, bf16[1,128,4096]{2,1,0:T(8,128)(2,1)}, u32[]{:S(2)}) %copy-start) | copy-done | bytes 1048600
  2.5 0.0 copy-start.1
  2.5 1.2 %copy-done.1 = bf16[1,128,4096]{2,1,0:T(8,128)(2,1)S(1)} copy-done((bf16[1,128,4096]{2,1,0:T(8,128)(2,1)S(1)}, bf16[1,128,4096]{2,1,0:T(8,128)(2,1)}, u32[]{:S(2)}) %copy-start.1) | copy-done | bytes 1048600
  3.8 0.0 copy-start.2
  3.8 0.9 %copy-done.2 = bf16[1,128,512]{2,1,0:T(8,128)(2,1)S(1)} copy-done((bf16[1,128,512]{2,1,0:T(8,128)(2,1)S(1)}, bf16[1,128,512]{2,1,0:T(8,128)(2,1)}, u32[]{:S(2)}) %copy-start.2) | copy-done | bytes 131096
  4.7 0.0 copy-start.3
  4.7 0.9 %copy-done.3 = bf16[1,128,512]{2,1,0:T(8,128)(2,1)S(1)} copy-done((bf16[1,128,512]{2,1,0:T(8,128)(2,1)S(1)}, bf16[1,128,512]{2,1,0:T(8,128)(2,1)}, u32[]{:S(2)}) %copy-start.3) | copy-done | bytes 131096
  5.6 71.0 %shard_map.110 = (bf16[1,128,4096]{2,1,0:T(8,128)(2,1)S(1)}, bf16[1,128,512]{2,1,0:T(8,128)(2,1)S(1)}, bf16[1,128,512]{2,1,0:T(8,128)(2,1)S(1)}, f32[1,128]{1,0:T(1,128)S(1)}, f32[1,128]{1,0:T(1,128)S(1)}) custom-call(s32[1,8]{1,0:T(1,128)S(1)} %copy-done.4, bf16[1,128,4096]{2,1,0:T(8,128)(2,1)S(1)} %copy-done, bf16[1,128,512]{2,1,0:T(8,128)(2,1)S(1)} %copy-done.2, ...), custom_call_target="tpu_custom_call" | custom-call | tf_op jit(solution)/shard_map/pallas_call | solution.py:491
  76.6 1.0 %copy.17 = bf16[1,128,4096]{2,1,0:T(8,128)(2,1)} copy(bf16[1,128,4096]{2,1,0:T(8,128)(2,1)S(1)} %get-tuple-element.20) | data formatting | bytes 2097152
  77.6 0.7 copy.18
  78.2 0.7 copy.19
  78.9 0.5 copy.20
  79.4 0.5 copy.21
Async XLA Ops:
  0.6 0.7 copy-start.4
  0.6 0.7 copy-start.5
  0.7 0.7 copy-start.6
  1.3 1.2 %copy-start = (bf16[1,128,4096]{2,1,0:T(8,128)(2,1)S(1)}, bf16[1,128,4096]{2,1,0:T(8,128)(2,1)}, u32[]{:S(2)}) copy-start(bf16[1,128,4096]{2,1,0:T(8,128)(2,1)} %q_hbm.1) | copy-start | bytes 3145732
  2.5 1.2 %copy-start.1 = (bf16[1,128,4096]{2,1,0:T(8,128)(2,1)S(1)}, bf16[1,128,4096]{2,1,0:T(8,128)(2,1)}, u32[]{:S(2)}) copy-start(bf16[1,128,4096]{2,1,0:T(8,128)(2,1)} %g_hbm.1) | copy-start | bytes 3145732
  3.8 0.9 %copy-start.2 = (bf16[1,128,512]{2,1,0:T(8,128)(2,1)S(1)}, bf16[1,128,512]{2,1,0:T(8,128)(2,1)}, u32[]{:S(2)}) copy-start(bf16[1,128,512]{2,1,0:T(8,128)(2,1)} %k_hbm.1) | copy-start | bytes 393220
  4.7 0.9 %copy-start.3 = (bf16[1,128,512]{2,1,0:T(8,128)(2,1)S(1)}, bf16[1,128,512]{2,1,0:T(8,128)(2,1)}, u32[]{:S(2)}) copy-start(bf16[1,128,512]{2,1,0:T(8,128)(2,1)} %v_hbm.1) | copy-start | bytes 393220
where the time goes:
time: 80.2 us; the launch traced here: 79.9 us
  Pallas kernels  71 us (89%)
  local copies, waits for them, and re-layouts  8.22 us (10%)
    pallas_call x1, Pallas kernels, on_device(): pl.pallas_call(kernel, out_shape=(jax.ShapeDtypeStruct(queries.shape, BF)...  71 us
    unnamed x19, local copies, waits for them, and re-layouts  8.22 us

commit v1 on v0

v1 whole, which is shorter than its diff:
```python
import math

import jax
import jax.numpy as jnp
from jax import lax
from jax.experimental import pallas as pl
from jax.experimental.pallas import tpu as pltpu
from jax.sharding import PartitionSpec as P

HK = 4
HD = 128
T = 128
KEYS = 8 * T
ROWS = 16 * T
EPS = 1e-06
SCALE = 1.0 / math.sqrt(HD)
EXP2_SCALE = SCALE * math.log2(math.e)
NEG = -1e30
BF = jnp.bfloat16
F32 = jnp.float32
MESH = pl.DeviceIdType.MESH
NT = (((1,), (1,)), ((), ()))
NN = (((1,), (0,)), ((), ()))

STEP_FORWARD = 6
STEP_REDUCE = 6
EARLY = 4


def dot(a, b, dims):
    return lax.dot_general(a, b, dims, preferred_element_type=F32)


def make_bias(bias, order, chip, core):
    keys_at = lax.broadcasted_iota(jnp.int32, (T, T), 0)
    rows_at = lax.broadcasted_iota(jnp.int32, (T, T), 1)
    for rel in range(2):
        own = order[0, 2 * chip + (core if rel == 0 else 1 - core)]
        for j in range(8):
            block = order[0, 2 * lax.rem(chip + j // 2, 4) + j % 2]
            bias[rel, j] = jnp.where(block * T + keys_at <= own * T + rows_at, 0.0, NEG)


def prepare(u, rel, hp, q_buf, g_buf, q_normed, g_cols, q_unit, q_factor, gain_cols):
    cols = pl.ds(pl.multiple_of(hp * 256, 256), 256)
    out = pl.ds(pl.multiple_of(rel * 1024 + hp * 256, 256), 256)
    q2 = q_buf[u, rel, :, cols].astype(F32)
    g2 = g_buf[u, rel, :, cols].astype(F32)
    q = jnp.concatenate([q2[:, :HD].T, q2[:, HD:].T], 1)
    factor = lax.rsqrt(jnp.mean(q * q, 0, keepdims=True) + EPS)
    unit = q * factor
    q_factor[u, :, out] = jnp.broadcast_to(factor, (8, 256))
    q_unit[u, :, out] = unit
    q_normed[u, :, out] = (unit * gain_cols[...]).astype(BF)
    g_cols[u, :, out] = jnp.concatenate([g2[:, :HD].T, g2[:, HD:].T], 1).astype(BF)


def softmax_part(u, r, kv, q_normed, g_cols, bias, e_all, x_all, stat, w_all):
    rel = r // 4
    cols = pl.ds(pl.multiple_of(r * 256, 256), 256)
    qn = q_normed[u, :, cols]
    g = g_cols[u, :, cols]
    total = jnp.zeros((8, 256), F32)
    cross = jnp.zeros((8, 256), F32)
    half = T // 2
    for j in range(0, 8, 2):
        s = dot(kv[u, 0, j : j + 2].reshape(2 * T, HD), qn, NN)
        d = dot(kv[u, 1, j : j + 2].reshape(2 * T, HD), g, NN)
        for b in range(4):
            at, row = b * half, j * T + b * half
            tile = bias[rel, j + b // 2, (b % 2) * half : (b % 2 + 1) * half, :]
            tile = jnp.concatenate([tile, tile], 1)
            e = jnp.exp2(s[at : at + half] * EXP2_SCALE + tile)
            x = e * d[at : at + half]
            total = total + jnp.sum(e.reshape(half // 8, 8, 256), 0)
            cross = cross + jnp.sum(x.reshape(half // 8, 8, 256), 0)
            e_all[u, row : row + half, cols] = e.astype(BF)
            x_all[u, row : row + half, cols] = x.astype(BF)
    inv = 1.0 / jnp.sum(total, 0, keepdims=True)
    row_dots = jnp.sum(cross, 0, keepdims=True) * inv
    stat[u, 0, :, cols] = jnp.broadcast_to(inv * SCALE, (8, 256))
    stat[u, 1, :, cols] = jnp.broadcast_to(row_dots, (8, 256))
    scaled = qn.astype(F32) * inv
    w_all[u, 0:128, cols] = (g.astype(F32) * inv).astype(BF)
    w_all[u, 128:256, cols] = (scaled * -row_dots).astype(BF)
    w_all[u, 256:384, cols] = scaled.astype(BF)


def key_part(u, slot, e_all, x_all, w_all):
    at = slice(slot * 256, slot * 256 + 256)
    both = dot(e_all[u, at, :], w_all[u, 0:256, :], NT)
    dk = (both[:, HD:] + dot(x_all[u, at, :], w_all[u, 256:384, :], NT)) * SCALE
    return dk, both[:, :HD]


def query_part(u, r, kt, e_all, x_all, stat, q_unit, q_factor, gain_cols, dq_buf, gain_acc):
    rel = r // 2
    rows = pl.ds(pl.multiple_of(r * 512, 512), 512)
    x = dot(kt[u], x_all[u, :, rows], NN)
    e = dot(kt[u], e_all[u, :, rows], NN)
    dq = (x - e * stat[u, 1, 0:1, rows]) * stat[u, 0, 0:1, rows]
    unit = q_unit[u, :, rows]
    prod = dq * unit
    gain_acc[...] += (prod[:, :HD] + prod[:, HD:256]) + (prod[:, 256:384] + prod[:, 384:])
    gain = gain_cols[...]
    scaled = dq * jnp.concatenate([gain, gain], 1)
    mean = jnp.mean(scaled * unit, 0, keepdims=True)
    out = q_factor[u, 0:1, rows] * (scaled - unit * mean)
    cols = pl.ds(pl.multiple_of((r % 2) * 512, 512), 512)
    dq_buf[u, rel, :, cols] = jnp.concatenate([out[:, i * HD : i * HD + HD].T for i in range(4)], 1).astype(BF)


def kernel(
    order,
    q_hbm,
    k_hbm,
    v_hbm,
    q_gain,
    k_gain,
    g_hbm,
    dq_hbm,
    dk_hbm,
    dv_hbm,
    gains_out,
    k_in,
    v_in,
    q_buf,
    g_buf,
    q_normed,
    g_cols,
    q_unit,
    q_factor,
    gain_cols,
    own_kv,
    kv,
    kt,
    bias,
    e_all,
    x_all,
    stat,
    w_all,
    near_sum,
    own_sum,
    dq_buf,
    gain_acc,
    k_gain_acc,
    b1_out,
    b1_in,
    b2_out,
    b2_in,
    sib_out,
    sib_in,
    dk_buf,
    dv_buf,
    ga_in,
    gb_in,
    load_sem,
    qx_send,
    qx_recv,
    s1_send,
    s1_recv,
    s2_send,
    s2_recv,
    sk_send,
    sk_recv,
    b1_send,
    b1_recv,
    b2_send,
    b2_recv,
    sb_send,
    sb_recv,
    out_sem,
    ox_send,
    ox_recv,
    ga_send,
    ga_recv,
    gb_send,
    gb_recv,
    fin_sem,
):
    ctx = lax.axis_index("ctx")
    dp = lax.axis_index("dp")
    chip = ctx // 2
    core = ctx % 2
    other = 1 - core
    sibling = 2 * chip + other
    near = (lax.rem(chip + 1, 4), lax.rem(chip + 3, 4))
    dp_z = dp % 2
    dp_xy = dp // 2
    ring_at = dp_z * 8 + ctx

    def ring_peer(m):
        return {"dp": dp_xy * 2 + m // 8, "ctx": m % 8}

    def plane_peer(m):
        return {"dp": m * 2 + dp_z}

    def remote(src, dst, ssem, rsem, dev):
        return pltpu.make_async_remote_copy(
            src_ref=src, dst_ref=dst, send_sem=ssem, recv_sem=rsem, device_id=dev, device_id_type=MESH
        )

    def head_cols(core_at, u):
        return pl.ds(pl.multiple_of(core_at * 2048 + u * 1024, 1024), 1024)

    barrier = pltpu.get_barrier_semaphore()

    def greet(r, carry):
        pl.semaphore_signal(barrier, inc=1, device_id=ring_peer(lax.rem(ring_at + r, 16)), device_id_type=MESH)
        pl.semaphore_signal(barrier, inc=1, device_id=plane_peer(lax.rem(dp_xy + r, 16)), device_id_type=MESH)
        return carry

    load_k = pltpu.make_async_copy(k_hbm.at[0], k_in, load_sem.at[0])
    load_v = pltpu.make_async_copy(v_hbm.at[0], v_in, load_sem.at[1])
    load_k.start()
    load_v.start()
    lax.fori_loop(1, 16, greet, 0)
    load_q = []
    for u in range(2):
        pair = (
            pltpu.make_async_copy(q_hbm.at[0, :, head_cols(core, u)], q_buf.at[u, 0], load_sem.at[2 + 2 * u]),
            pltpu.make_async_copy(g_hbm.at[0, :, head_cols(core, u)], g_buf.at[u, 0], load_sem.at[3 + 2 * u]),
        )
        load_q.append(pair)
        for c in pair:
            c.start()

    load_k.wait()
    load_v.wait()
    k_gain_row = k_gain[...]
    for h in range(HK):
        block = k_in[:, h * HD : (h + 1) * HD].astype(F32)
        factor = lax.rsqrt(jnp.mean(block * block, -1, keepdims=True) + EPS)
        own_kv[h, 0] = (block * factor * k_gain_row).astype(BF)
        own_kv[h, 1] = v_in[:, h * HD : (h + 1) * HD]

    pl.semaphore_wait(barrier, 30)

    lands = (3, 1)

    def stage1(u, d, dest_core, part):
        return remote(
            own_kv.at[2 * dest_core + u, part],
            kv.at[u, part, 2 * lands[d] + core],
            s1_send.at[u, d, dest_core, part],
            s1_recv.at[u, d, core, part],
            {"ctx": 2 * near[d] + dest_core},
        )

    def stage1_arrival(u, d, src_core, part):
        at = kv.at[u, part, 2 * lands[d] + src_core]
        return remote(at, at, s1_send.at[u, d, src_core, part], s1_recv.at[u, d, src_core, part], {"ctx": sibling})

    def sibling_kv(u):
        return remote(own_kv.at[2 * other + u], kv.at[u, :, core], sk_send.at[u], sk_recv.at[u], {"ctx": sibling})

    def sibling_kv_arrival(u):
        return remote(own_kv.at[2 * core + u], kv.at[u, :, other], sk_send.at[u], sk_recv.at[u], {"ctx": sibling})

    def stage2(u, d, src_core):
        return remote(
            kv.at[u, d, 2 * lands[d] + src_core],
            kv.at[u, d, 4 + src_core],
            s2_send.at[u, d, src_core],
            s2_recv.at[u, d, src_core],
            {"ctx": 2 * near[d] + core},
        )

    def stage2_arrival(u, d, src_core):
        at = kv.at[u, d, 4 + src_core]
        return remote(at, at, s2_send.at[u, d, src_core], s2_recv.at[u, d, src_core], {"ctx": sibling})

    def q_exchange(u):
        return (
            remote(q_hbm.at[0, :, head_cols(other, u)], q_buf.at[u, 1], qx_send.at[u, 0], qx_recv.at[u, 0], {"ctx": sibling}),
            remote(g_hbm.at[0, :, head_cols(other, u)], g_buf.at[u, 1], qx_send.at[u, 1], qx_recv.at[u, 1], {"ctx": sibling}),
        )

    def gather_start(u):
        for first in range(2):
            for d in range(2):
                for dest_core in range(2):
                    stage1(u, d, dest_core, d if first == 0 else 1 - d).start()
        sibling_kv(u).start()
        for c in q_exchange(u):
            c.start()

    def forward(u):
        for src_core in range(2):
            for d in range(2):
                stage1_arrival(u, d, src_core, d).wait_recv()
                stage2(u, d, src_core).start()

    def finish_gather(u):
        for src_core in range(2):
            for d in range(2):
                stage1_arrival(u, d, src_core, 1 - d).wait_recv()
        sibling_kv_arrival(u).wait_recv()
        for src_core in range(2):
            for d in range(2):
                stage2_arrival(u, d, src_core).wait_recv()
        kt[u] = kv[u, 0].reshape(KEYS, HD).T

    def prepare_rows(u, rel):
        if rel == 0:
            for c in load_q[u]:
                c.wait()
        else:
            for c in q_exchange(u):
                c.wait_recv()

        def one(hp, carry):
            prepare(u, rel, hp, q_buf, g_buf, q_normed, g_cols, q_unit, q_factor, gain_cols)
            return carry

        lax.fori_loop(0, 4, one, 0)

    def b1(u, d):
        return remote(b1_out.at[u, d], b1_in.at[u, d], b1_send.at[u, d], b1_recv.at[u, d], {"ctx": 2 * near[d] + core})

    def b2(u, d, dest_core, part):
        return remote(
            b2_out.at[u, d, dest_core, part],
            b2_in.at[u, d, core, part],
            b2_send.at[u, d, dest_core, part],
            b2_recv.at[u, d, core, part],
            {"ctx": 2 * near[d] + dest_core},
        )

    def b2_arrival(u, d, src_core, part):
        at = b2_in.at[u, d, src_core, part]
        return remote(at, at, b2_send.at[u, d, src_core, part], b2_recv.at[u, d, src_core, part], {"ctx": sibling})

    def sibling_sum(u):
        return remote(sib_out.at[u], sib_in.at[u], sb_send.at[u], sb_recv.at[u], {"ctx": sibling})

    def key_sums(u, slot):
        sums = key_part(u, slot, e_all, x_all, w_all)
        k_rows = kv[u, 0, 2 * slot : 2 * slot + 2].reshape(2 * T, HD).astype(F32)
        k_gain_acc[...] += jnp.sum((sums[0] * k_rows).reshape(32, 8, HD), 0)
        return sums

    def reduce_start(u):
        sums = key_sums(u, 2)
        for d in range(2):
            b1_out[u, d] = sums[d].reshape(2, T, HD).astype(BF)
            b1(u, d).start()
        for d, slot in ((0, 1), (1, 3)):
            sums = key_sums(u, slot)
            for dest_core in range(2):
                b2_out[u, d, dest_core, 1 - d] = sums[1 - d][dest_core * T : dest_core * T + T].astype(BF)
                b2(u, d, dest_core, 1 - d).start()
            near_sum[u, d] = sums[d].reshape(2, T, HD)
        sums = key_sums(u, 0)
        for part in range(2):
            own_sum[u, part] = sums[part].reshape(2, T, HD)
            sib_out[u, part] = own_sum[u, part, other].astype(BF)
        sibling_sum(u).start()

    def reduce_middle(u):
        for d in range(2):
            b1(u, d).wait_recv()
            for dest_core in range(2):
                b2_out[u, d, dest_core, d] = (near_sum[u, d, dest_core] + b1_in[u, d, dest_core].astype(F32)).astype(BF)
                b2(u, d, dest_core, d).start()

    def reduce_finish(u):
        sibling_sum(u).wait_recv()
        for d in range(2):
            for src_core in range(2):
                for part in range(2):
                    b2_arrival(u, d, src_core, part).wait_recv()
        for rel in range(2):
            at = core if rel == 0 else other
            sums = []
            for part in range(2):
                own = own_sum[u, part, core] if rel == 0 else sib_in[u, part].astype(F32)
                sums.append(own + b2_in[u, 0, at, part].astype(F32) + b2_in[u, 1, at, part].astype(F32))
            cols = pl.ds(pl.multiple_of(at * 256 + u * HD, HD), HD)
            block = k_in[:, cols].astype(F32)
            factor = lax.rsqrt(jnp.mean(block * block, -1, keepdims=True) + EPS)
            unit = block * factor
            scaled = sums[0] * k_gain_row
            mean = jnp.mean(scaled * unit, -1, keepdims=True)
            dk_buf[:, cols] = (factor * (scaled - unit * mean)).astype(BF)
            dv_buf[:, cols] = sums[1].astype(BF)

    def out_local(u):
        return pltpu.make_async_copy(dq_buf.at[u, 0], dq_hbm.at[0, :, head_cols(core, u)], out_sem.at[u])

    def out_remote(u):
        return remote(dq_buf.at[u, 1], dq_hbm.at[0, :, head_cols(core, u)], ox_send.at[u], ox_recv.at[u], {"ctx": sibling})

    def out_arrival(u):
        return remote(dq_buf.at[u, 1], dq_hbm.at[0, :, head_cols(other, u)], ox_send.at[u], ox_recv.at[u], {"ctx": sibling})

    def softmax_parts(u, hook_at, hook):
        def one(r, carry):
            @pl.when(r == hook_at)
            def _():
                hook()

            softmax_part(u, r, kv, q_normed, g_cols, bias, e_all, x_all, stat, w_all)
            return carry

        lax.fori_loop(0, 8, one, 0)

    def query_parts(u, lo, hi):
        def one(r, carry):
            query_part(u, r, kt, e_all, x_all, stat, q_unit, q_factor, gain_cols, dq_buf, gain_acc)
            return carry

        lax.fori_loop(lo, hi, one, 0)

    gather_start(0)
    for u in range(2):
        for part in range(2):
            kv[u, part, core] = own_kv[2 * core + u, part]
    column = jnp.broadcast_to(q_gain[...], (HD, HD)).T
    gain_cols[...] = jnp.concatenate([column, column], 1)
    gain_acc[...] = jnp.zeros_like(gain_acc)
    k_gain_acc[...] = jnp.zeros_like(k_gain_acc)
    make_bias(bias, order, chip, core)
    prepare_rows(0, 0)
    forward(0)
    gather_start(1)
    prepare_rows(1, 0)
    prepare_rows(0, 1)
    finish_gather(0)
    softmax_parts(0, STEP_FORWARD, lambda: forward(1))
    reduce_start(0)
    query_parts(0, 0, EARLY)
    out_local(0).start()
    out_remote(0).start()
    prepare_rows(1, 1)
    finish_gather(1)
    softmax_parts(1, STEP_REDUCE, lambda: reduce_middle(0))
    reduce_start(1)
    query_parts(1, 0, 4)
    out_local(1).start()
    out_remote(1).start()

    def ga(r):
        return remote(ga_in.at[ring_at], ga_in.at[ring_at], ga_send.at[r], ga_recv.at[ring_at], ring_peer(lax.rem(ring_at + r, 16)))

    def ga_arrival(r):
        j = lax.rem(ring_at + r, 16)
        return remote(ga_in.at[j], ga_in.at[j], ga_send.at[r], ga_recv.at[j], {"ctx": sibling})

    def gb(r):
        return remote(gb_in.at[dp_xy], gb_in.at[dp_xy], gb_send.at[r], gb_recv.at[dp_xy], plane_peer(lax.rem(dp_xy + r, 16)))

    def gb_arrival(r):
        j = lax.rem(dp_xy + r, 16)
        return remote(gb_in.at[j], gb_in.at[j], gb_send.at[r], gb_recv.at[j], {"ctx": sibling})

    def for_peers(act):
        def one(r, carry):
            act(r)
            return carry

        lax.fori_loop(1, 16, one, 0)

    ga_in[ring_at, 0] = jnp.sum(gain_acc[...].T.reshape(16, 8, HD), 0)
    ga_in[ring_at, 1] = k_gain_acc[...]
    for_peers(lambda r: ga(r).start())
    reduce_middle(1)
    for_peers(lambda r: ga_arrival(r).wait_recv())
    gb_in[dp_xy] = jnp.sum(ga_in[...], 0)
    for_peers(lambda r: gb(r).start())
    reduce_finish(0)
    reduce_finish(1)
    fin_k = pltpu.make_async_copy(dk_buf, dk_hbm.at[0], fin_sem.at[0])
    fin_v = pltpu.make_async_copy(dv_buf, dv_hbm.at[0], fin_sem.at[1])
    fin_k.start()
    fin_v.start()
    for_peers(lambda r: gb_arrival(r).wait_recv())
    gains = jnp.sum(jnp.sum(gb_in[...], 0), 1, keepdims=True)
    gains_out[0:1] = gains[0]
    gains_out[1:2] = gains[1] / k_gain_row

    for u in range(2):
        for d in range(2):
            for dest_core in range(2):
                for part in range(2):
                    stage1(u, d, dest_core, part).wait_send()
                    b2(u, d, dest_core, part).wait_send()
                stage2(u, d, dest_core).wait_send()
            b1(u, d).wait_send()
        sibling_kv(u).wait_send()
        sibling_sum(u).wait_send()
        for c in q_exchange(u):
            c.wait_send()
        out_local(u).wait()
        out_remote(u).wait_send()
        out_arrival(u).wait_recv()
    for_peers(lambda r: ga(r).wait_send())
    for_peers(lambda r: gb(r).wait_send())
    fin_k.wait()
    fin_v.wait()


def settle(dq, dk, dv, gains, dq_out, dk_out, dv_out, q_gain_out, k_gain_out, dq_mid, dk_mid, dv_mid, gains_mid, in_sem, out_sem):
    parts = [(gains, gains_mid), (dk, dk_mid), (dv, dv_mid)]
    outs = [(gains_mid.at[0], q_gain_out), (gains_mid.at[1], k_gain_out), (dk_mid, dk_out), (dv_mid, dv_out)]
    for i in range(4):
        rows = pl.ds(i * 32, 32)
        parts.append((dq.at[0, rows], dq_mid.at[0, rows]))
        outs.append((dq_mid.at[0, rows], dq_out.at[0, rows]))
    loads = [pltpu.make_async_copy(a, b, in_sem.at[i]) for i, (a, b) in enumerate(parts)]
    stores = [pltpu.make_async_copy(a, b, out_sem.at[i]) for i, (a, b) in enumerate(outs)]
    for c in loads:
        c.start()
    loads[0].wait()
    stores[0].start()
    for i in range(1, 7):
        loads[i].wait()
        stores[i + 1].start()
    stores[1].start()
    for c in stores:
        c.wait()


def on_device(queries, keys, values, q_gain, k_gain, out_grad, block_order):
    hbm = pl.BlockSpec(memory_space=pl.ANY)
    vmem = pl.BlockSpec(memory_space=pltpu.VMEM)
    smem = pl.BlockSpec(memory_space=pltpu.SMEM)
    dma = pltpu.SemaphoreType.DMA
    sends = [dma((2, 2)), dma((2, 2, 2, 2)), dma((2, 2, 2)), dma((2,)), dma((2, 2)), dma((2, 2, 2, 2)), dma((2,))]
    results = pl.pallas_call(
        kernel,
        out_shape=(
            jax.ShapeDtypeStruct(queries.shape, BF),
            jax.ShapeDtypeStruct(keys.shape, BF),
            jax.ShapeDtypeStruct(values.shape, BF),
            jax.ShapeDtypeStruct((2, HD), F32),
        ),
        in_specs=[smem, hbm, hbm, hbm, vmem, vmem, hbm],
        out_specs=(hbm, hbm, hbm, vmem),
        scratch_shapes=[
            pltpu.VMEM((T, HK * HD), BF),
            pltpu.VMEM((T, HK * HD), BF),
            pltpu.VMEM((2, 2, T, 1024), BF),
            pltpu.VMEM((2, 2, T, 1024), BF),
            pltpu.VMEM((2, HD, ROWS), BF),
            pltpu.VMEM((2, HD, ROWS), BF),
            pltpu.VMEM((2, HD, ROWS), F32),
            pltpu.VMEM((2, 8, ROWS), F32),
            pltpu.VMEM((HD, 256), F32),
            pltpu.VMEM((HK, 2, T, HD), BF),
            pltpu.VMEM((2, 2, 8, T, HD), BF),
            pltpu.VMEM((2, HD, KEYS), BF),
            pltpu.VMEM((2, 8, T, T), F32),
            pltpu.VMEM((2, KEYS, ROWS), BF),
            pltpu.VMEM((2, KEYS, ROWS), BF),
            pltpu.VMEM((2, 2, 8, ROWS), F32),
            pltpu.VMEM((2, 3 * HD, ROWS), BF),
            pltpu.VMEM((2, 2, 2, T, HD), F32),
            pltpu.VMEM((2, 2, 2, T, HD), F32),
            pltpu.VMEM((2, 2, T, 1024), BF),
            pltpu.VMEM((HD, HD), F32),
            pltpu.VMEM((8, HD), F32),
            pltpu.VMEM((2, 2, 2, T, HD), BF),
            pltpu.VMEM((2, 2, 2, T, HD), BF),
            pltpu.VMEM((2, 2, 2, 2, T, HD), BF),
            pltpu.VMEM((2, 2, 2, 2, T, HD), BF),
            pltpu.VMEM((2, 2, T, HD), BF),
            pltpu.VMEM((2, 2, T, HD), BF),
            pltpu.VMEM((T, HK * HD), BF),
            pltpu.VMEM((T, HK * HD), BF),
            pltpu.VMEM((16, 2, 8, HD), F32),
            pltpu.VMEM((16, 2, 8, HD), F32),
            dma((6,)),
        ]
        + [s for s in sends for _ in range(2)]
        + [dma((2,)), dma((2,)), dma((2,))]
        + [dma((16,)) for _ in range(4)]
        + [dma((2,))],
        compiler_params=pltpu.CompilerParams(
            collective_id=0, has_side_effects=True, vmem_limit_bytes=60 * 1024 * 1024
        ),
    )(block_order, queries, keys, values, q_gain.reshape(1, HD), k_gain.reshape(1, HD), out_grad)
    return pl.pallas_call(
        settle,
        out_shape=(
            jax.ShapeDtypeStruct(queries.shape, BF),
            jax.ShapeDtypeStruct(keys.shape, BF),
            jax.ShapeDtypeStruct(values.shape, BF),
            jax.ShapeDtypeStruct((HD,), F32),
            jax.ShapeDtypeStruct((HD,), F32),
        ),
        in_specs=[hbm] * 4,
        out_specs=(hbm,) * 5,
        scratch_shapes=[
            pltpu.VMEM((1, T, 32 * HD), BF),
            pltpu.VMEM((1, T, HK * HD), BF),
            pltpu.VMEM((1, T, HK * HD), BF),
            pltpu.VMEM((2, HD), F32),
            dma((7,)),
            dma((8,)),
        ],
        compiler_params=pltpu.CompilerParams(vmem_limit_bytes=60 * 1024 * 1024),
    )(*results)


def solution(mesh):
    placed = (
        P("dp", "ctx", None),
        P("dp", "ctx", None),
        P("dp", "ctx", None),
        P(),
        P(),
        P("dp", "ctx", None),
        P("dp", None),
    )
    return jax.shard_map(
        on_device,
        mesh=mesh,
        in_specs=placed,
        out_specs=(P("dp", "ctx", None), P("dp", "ctx", None), P("dp", "ctx", None), P(), P()),
        check_vma=False,
    )
```

time: 80.2 us -> 63.4 us (0.79)
  Pallas kernels: 71 us -> 62.7 us
  local copies, waits for them, and re-layouts: 8.22 us -> 0 us
    pallas_call x1, Pallas kernels: 71 us -> 60.5 us  [on_device(): pl.pallas_call(kernel, out_shape=(jax.ShapeDtypeStruct(queries.shape, BF)...]
    unnamed x19 -> x0, local copies, waits for them, and re-layouts: 8.22 us -> none
    pallas_call x0 -> x1, Pallas kernels: none -> 2.18 us  [on_device(): pl.pallas_call(settle, out_shape=(jax.ShapeDtypeStruct(queries.shape, BF)...]
where the time goes in v1:
time: 63.4 us; the launch traced here: 63.3 us
  Pallas kernels  62.7 us (99%)
  between operations  0.64 us (1%)
    pallas_call x1, Pallas kernels, on_device(): pl.pallas_call(kernel, out_shape=(jax.ShapeDtypeStruct(queries.shape, BF)...  60.5 us
    pallas_call x1, Pallas kernels, on_device(): pl.pallas_call(settle, out_shape=(jax.ShapeDtypeStruct(queries.shape, BF)...  2.18 us

profile of v1, /device:TPU:1, one launch (start us, length us, event | category | flops | bytes accessed | tf_op | source)
XLA Modules:
  0.0 63.3 jit_solution(14534497893367462892)
XLA Ops:
  0.6 60.5 %shard_map.110 = (bf16[1,128,4096]{2,1,0:T(8,128)(2,1)}, bf16[1,128,512]{2,1,0:T(8,128)(2,1)}, bf16[1,128,512]{2,1,0:T(8,128)(2,1)}, f32[2,128]{1,0:T(2,128)}) custom-call(s32[1,8]{1,0:T(1,128)} %order.1, bf16[1,128,4096]{2,1,0:T(8,128)(2,1)} %q_hbm.1, bf16[1,128,512]{2,1,0:T(8,128)(2,1)} %k_hbm.1, bf16[1,128,512]{2,1,0:T(8,128)(2,1)} %v_hbm.1, ...), custom_call_target="tpu_custom_call" | custom-call | tf_op jit(solution)/shard_map/pallas_call | solution.py:530
  61.1 2.2 %shard_map.111 = (bf16[1,128,4096]{2,1,0:T(8,128)(2,1)}, bf16[1,128,512]{2,1,0:T(8,128)(2,1)}, bf16[1,128,512]{2,1,0:T(8,128)(2,1)}, f32[128]{0:T(128)}, f32[128]{0:T(128)}) custom-call(bf16[1,128,4096]{2,1,0:T(8,128)(2,1)} %get-tuple-element.9.dq, bf16[1,128,512]{2,1,0:T(8,128)(2,1)} %get-tuple-element.10.dk, bf16[1,128,512]{2,1,0:T(8,128)(2,1)} %get-tuple-element.11.dv, ...), custom_call_target="tpu_custom_call" | custom-call | tf_op jit(solution)/shard_map/pallas_call | solution.py:583

commit v2 on v1

--- a/solution.py
+++ b/solution.py
@@ -1,3 +1,4 @@
+import functools
 import math
 
 import jax
@@ -22,9 +23,8 @@
 NT = (((1,), (1,)), ((), ()))
 NN = (((1,), (0,)), ((), ()))
 
-STEP_FORWARD = 6
-STEP_REDUCE = 6
-EARLY = 4
+STEPS_FORWARD = (4, 7)
+STEPS_REDUCE = (4, 7)
 
 
 def dot(a, b, dims):
@@ -93,15 +93,13 @@
     return dk, both[:, :HD]
 
 
-def query_part(u, r, kt, e_all, x_all, stat, q_unit, q_factor, gain_cols, dq_buf, gain_acc):
+def query_part(u, r, kt, e_all, x_all, stat, q_unit, q_factor, gain_cols, dq_buf):
     rel = r // 2
     rows = pl.ds(pl.multiple_of(r * 512, 512), 512)
     x = dot(kt[u], x_all[u, :, rows], NN)
     e = dot(kt[u], e_all[u, :, rows], NN)
     dq = (x - e * stat[u, 1, 0:1, rows]) * stat[u, 0, 0:1, rows]
     unit = q_unit[u, :, rows]
-    prod = dq * unit
-    gain_acc[...] += (prod[:, :HD] + prod[:, HD:256]) + (prod[:, 256:384] + prod[:, 384:])
     gain = gain_cols[...]
     scaled = dq * jnp.concatenate([gain, gain], 1)
     mean = jnp.mean(scaled * unit, 0, keepdims=True)
@@ -111,16 +109,20 @@
 
 
 def kernel(
-    order,
+    order_hbm,
     q_hbm,
     k_hbm,
     v_hbm,
-    q_gain,
-    k_gain,
+    q_gain_hbm,
+    k_gain_hbm,
     g_hbm,
     dq_hbm,
     dk_hbm,
     dv_hbm,
+    gains_hbm,
+    order,
+    q_gain,
+    k_gain,
     gains_out,
     k_in,
     v_in,
@@ -143,7 +145,6 @@
     own_sum,
     dq_buf,
     gain_acc,
-    k_gain_acc,
     b1_out,
     b1_in,
     b2_out,
@@ -210,11 +211,16 @@
         pl.semaphore_signal(barrier, inc=1, device_id=plane_peer(lax.rem(dp_xy + r, 16)), device_id_type=MESH)
         return carry
 
-    load_k = pltpu.make_async_copy(k_hbm.at[0], k_in, load_sem.at[0])
-    load_v = pltpu.make_async_copy(v_hbm.at[0], v_in, load_sem.at[1])
-    load_k.start()
-    load_v.start()
     lax.fori_loop(1, 16, greet, 0)
+    loads = [
+        pltpu.make_async_copy(k_hbm.at[0], k_in, load_sem.at[0]),
+        pltpu.make_async_copy(k_gain_hbm, k_gain, load_sem.at[6]),
+        pltpu.make_async_copy(v_hbm.at[0], v_in, load_sem.at[1]),
+        pltpu.make_async_copy(q_gain_hbm, q_gain, load_sem.at[7]),
+        pltpu.make_async_copy(order_hbm, order, load_sem.at[8]),
+    ]
+    for c in loads:
+        c.start()
     load_q = []
     for u in range(2):
         pair = (
@@ -225,8 +231,8 @@
         for c in pair:
             c.start()
 
-    load_k.wait()
-    load_v.wait()
+    for c in loads:
+        c.wait()
     k_gain_row = k_gain[...]
     for h in range(HK):
         block = k_in[:, h * HD : (h + 1) * HD].astype(F32)
@@ -276,20 +282,23 @@
             remote(g_hbm.at[0, :, head_cols(other, u)], g_buf.at[u, 1], qx_send.at[u, 1], qx_recv.at[u, 1], {"ctx": sibling}),
         )
 
-    def gather_start(u):
-        for first in range(2):
-            for d in range(2):
-                for dest_core in range(2):
-                    stage1(u, d, dest_core, d if first == 0 else 1 - d).start()
+    by_core = (core, other)
+
+    def share(u):
         sibling_kv(u).start()
         for c in q_exchange(u):
             c.start()
 
-    def forward(u):
-        for src_core in range(2):
-            for d in range(2):
-                stage1_arrival(u, d, src_core, d).wait_recv()
-                stage2(u, d, src_core).start()
+    def gather_start(u):
+        for first in range(2):
+            for dest_core in by_core:
+                for d in range(2):
+                    stage1(u, d, dest_core, d if first == 0 else 1 - d).start()
+
+    def forward(u, src_core):
+        for d in range(2):
+            stage1_arrival(u, d, src_core, d).wait_recv()
+            stage2(u, d, src_core).start()
 
     def finish_gather(u):
         for src_core in range(2):
@@ -315,8 +324,10 @@
 
         lax.fori_loop(0, 4, one, 0)
 
-    def b1(u, d):
-        return remote(b1_out.at[u, d], b1_in.at[u, d], b1_send.at[u, d], b1_recv.at[u, d], {"ctx": 2 * near[d] + core})
+    def b1(u, d, kk):
+        return remote(
+            b1_out.at[u, d, kk], b1_in.at[u, d, kk], b1_send.at[u, d, kk], b1_recv.at[u, d, kk], {"ctx": 2 * near[d] + core}
+        )
 
     def b2(u, d, dest_core, part):
         return remote(
@@ -337,14 +348,16 @@
     def key_sums(u, slot):
         sums = key_part(u, slot, e_all, x_all, w_all)
         k_rows = kv[u, 0, 2 * slot : 2 * slot + 2].reshape(2 * T, HD).astype(F32)
-        k_gain_acc[...] += jnp.sum((sums[0] * k_rows).reshape(32, 8, HD), 0)
+        gain_acc[...] += jnp.sum((sums[0] * k_rows).reshape(32, 8, HD), 0)
         return sums
 
     def reduce_start(u):
         sums = key_sums(u, 2)
         for d in range(2):
             b1_out[u, d] = sums[d].reshape(2, T, HD).astype(BF)
-            b1(u, d).start()
+        for kk in range(2):
+            for d in range(2):
+                b1(u, d, kk).start()
         for d, slot in ((0, 1), (1, 3)):
             sums = key_sums(u, slot)
             for dest_core in range(2):
@@ -357,12 +370,11 @@
             sib_out[u, part] = own_sum[u, part, other].astype(BF)
         sibling_sum(u).start()
 
-    def reduce_middle(u):
+    def reduce_middle(u, kk):
         for d in range(2):
-            b1(u, d).wait_recv()
-            for dest_core in range(2):
-                b2_out[u, d, dest_core, d] = (near_sum[u, d, dest_core] + b1_in[u, d, dest_core].astype(F32)).astype(BF)
-                b2(u, d, dest_core, d).start()
+            b1(u, d, kk).wait_recv()
+            b2_out[u, d, kk, d] = (near_sum[u, d, kk] + b1_in[u, d, kk].astype(F32)).astype(BF)
+            b2(u, d, kk, d).start()
 
     def reduce_finish(u):
         sibling_sum(u).wait_recv()
@@ -394,11 +406,10 @@
     def out_arrival(u):
         return remote(dq_buf.at[u, 1], dq_hbm.at[0, :, head_cols(other, u)], ox_send.at[u], ox_recv.at[u], {"ctx": sibling})
 
-    def softmax_parts(u, hook_at, hook):
+    def softmax_parts(u, hooks):
         def one(r, carry):
-            @pl.when(r == hook_at)
-            def _():
-                hook()
+            for at, hook in hooks.items():
+                pl.when(r == at)(hook)
 
             softmax_part(u, r, kv, q_normed, g_cols, bias, e_all, x_all, stat, w_all)
             return carry
@@ -407,38 +418,37 @@
 
     def query_parts(u, lo, hi):
         def one(r, carry):
-            query_part(u, r, kt, e_all, x_all, stat, q_unit, q_factor, gain_cols, dq_buf, gain_acc)
+            query_part(u, r, kt, e_all, x_all, stat, q_unit, q_factor, gain_cols, dq_buf)
             return carry
 
         lax.fori_loop(lo, hi, one, 0)
 
     gather_start(0)
+    share(0)
+    share(1)
     for u in range(2):
         for part in range(2):
             kv[u, part, core] = own_kv[2 * core + u, part]
     column = jnp.broadcast_to(q_gain[...], (HD, HD)).T
     gain_cols[...] = jnp.concatenate([column, column], 1)
     gain_acc[...] = jnp.zeros_like(gain_acc)
-    k_gain_acc[...] = jnp.zeros_like(k_gain_acc)
     make_bias(bias, order, chip, core)
     prepare_rows(0, 0)
-    forward(0)
+    for at in by_core:
+        forward(0, at)
     gather_start(1)
     prepare_rows(1, 0)
     prepare_rows(0, 1)
+    prepare_rows(1, 1)
     finish_gather(0)
-    softmax_parts(0, STEP_FORWARD, lambda: forward(1))
+    softmax_parts(0, {at: functools.partial(forward, 1, k) for at, k in zip(STEPS_FORWARD, by_core)})
     reduce_start(0)
-    query_parts(0, 0, EARLY)
+    query_parts(0, 0, 4)
     out_local(0).start()
     out_remote(0).start()
-    prepare_rows(1, 1)
     finish_gather(1)
-    softmax_parts(1, STEP_REDUCE, lambda: reduce_middle(0))
+    softmax_parts(1, {at: functools.partial(reduce_middle, 0, k) for at, k in zip(STEPS_REDUCE, range(2))})
     reduce_start(1)
-    query_parts(1, 0, 4)
-    out_local(1).start()
-    out_remote(1).start()
 
     def ga(r):
         return remote(ga_in.at[ring_at], ga_in.at[ring_at], ga_send.at[r], ga_recv.at[ring_at], ring_peer(lax.rem(ring_at + r, 16)))
@@ -461,23 +471,28 @@
 
         lax.fori_loop(1, 16, one, 0)
 
-    ga_in[ring_at, 0] = jnp.sum(gain_acc[...].T.reshape(16, 8, HD), 0)
-    ga_in[ring_at, 1] = k_gain_acc[...]
+    gb_in[dp_xy] = jnp.sum(gain_acc[...], 0, keepdims=True)
+    for_peers(lambda r: gb(r).start())
+    query_parts(1, 0, 4)
+    out_local(1).start()
+    out_remote(1).start()
+    for_peers(lambda r: gb_arrival(r).wait_recv())
+    ga_in[ring_at] = jnp.sum(gb_in[...], 0)
     for_peers(lambda r: ga(r).start())
-    reduce_middle(1)
-    for_peers(lambda r: ga_arrival(r).wait_recv())
-    gb_in[dp_xy] = jnp.sum(ga_in[...], 0)
-    for_peers(lambda r: gb(r).start())
+    for kk in range(2):
+        reduce_middle(1, kk)
     reduce_finish(0)
     reduce_finish(1)
     fin_k = pltpu.make_async_copy(dk_buf, dk_hbm.at[0], fin_sem.at[0])
     fin_v = pltpu.make_async_copy(dv_buf, dv_hbm.at[0], fin_sem.at[1])
     fin_k.start()
     fin_v.start()
-    for_peers(lambda r: gb_arrival(r).wait_recv())
-    gains = jnp.sum(jnp.sum(gb_in[...], 0), 1, keepdims=True)
-    gains_out[0:1] = gains[0]
-    gains_out[1:2] = gains[1] / k_gain_row
+    for_peers(lambda r: ga_arrival(r).wait_recv())
+    gain_sum = jnp.sum(ga_in[...], 0)
+    gains_out[0:1] = gain_sum / q_gain[...]
+    gains_out[1:2] = gain_sum / k_gain_row
+    fin_g = pltpu.make_async_copy(gains_out, gains_hbm, fin_sem.at[2])
+    fin_g.start()
 
     for u in range(2):
         for d in range(2):
@@ -486,7 +501,8 @@
                     stage1(u, d, dest_core, part).wait_send()
                     b2(u, d, dest_core, part).wait_send()
                 stage2(u, d, dest_core).wait_send()
-            b1(u, d).wait_send()
+            for kk in range(2):
+                b1(u, d, kk).wait_send()
         sibling_kv(u).wait_send()
         sibling_sum(u).wait_send()
         for c in q_exchange(u):
@@ -498,35 +514,26 @@
     for_peers(lambda r: gb(r).wait_send())
     fin_k.wait()
     fin_v.wait()
-
-
-def settle(dq, dk, dv, gains, dq_out, dk_out, dv_out, q_gain_out, k_gain_out, dq_mid, dk_mid, dv_mid, gains_mid, in_sem, out_sem):
-    parts = [(gains, gains_mid), (dk, dk_mid), (dv, dv_mid)]
-    outs = [(gains_mid.at[0], q_gain_out), (gains_mid.at[1], k_gain_out), (dk_mid, dk_out), (dv_mid, dv_out)]
+    fin_g.wait()
+
+
+def settle(dq, dk, dv, gains, dq_out, dk_out, dv_out, q_gain_out, k_gain_out, sems):
+    pairs = [(gains.at[0], q_gain_out), (gains.at[1], k_gain_out), (dk, dk_out), (dv, dv_out)]
     for i in range(4):
         rows = pl.ds(i * 32, 32)
-        parts.append((dq.at[0, rows], dq_mid.at[0, rows]))
-        outs.append((dq_mid.at[0, rows], dq_out.at[0, rows]))
-    loads = [pltpu.make_async_copy(a, b, in_sem.at[i]) for i, (a, b) in enumerate(parts)]
-    stores = [pltpu.make_async_copy(a, b, out_sem.at[i]) for i, (a, b) in enumerate(outs)]
-    for c in loads:
+        pairs.append((dq.at[0, rows], dq_out.at[0, rows]))
+    copies = [pltpu.make_async_copy(a, b, sems.at[i]) for i, (a, b) in enumerate(pairs)]
+    for c in copies:
         c.start()
-    loads[0].wait()
-    stores[0].start()
-    for i in range(1, 7):
-        loads[i].wait()
-        stores[i + 1].start()
-    stores[1].start()
-    for c in stores:
+    for c in copies:
         c.wait()
 
 
 def on_device(queries, keys, values, q_gain, k_gain, out_grad, block_order):
     hbm = pl.BlockSpec(memory_space=pl.ANY)
-    vmem = pl.BlockSpec(memory_space=pltpu.VMEM)
-    smem = pl.BlockSpec(memory_space=pltpu.SMEM)
     dma = pltpu.SemaphoreType.DMA
-    sends = [dma((2, 2)), dma((2, 2, 2, 2)), dma((2, 2, 2)), dma((2,)), dma((2, 2)), dma((2, 2, 2, 2)), dma((2,))]
+    sends = [dma((2, 2)), dma((2, 2, 2, 2)), dma((2, 2, 2)), dma((2,)), dma((2, 2, 2)), dma((2, 2, 2, 2)), dma((2,))]
+    operands = (block_order, queries, keys, values, q_gain.reshape(1, HD), k_gain.reshape(1, HD), out_grad)
     results = pl.pallas_call(
         kernel,
         out_shape=(
@@ -535,9 +542,13 @@
             jax.ShapeDtypeStruct(values.shape, BF),
             jax.ShapeDtypeStruct((2, HD), F32),
         ),
-        in_specs=[smem, hbm, hbm, hbm, vmem, vmem, hbm],
-        out_specs=(hbm, hbm, hbm, vmem),
+        in_specs=[pl.BlockSpec(memory_space=pltpu.HBM)] * 7,
+        out_specs=(hbm,) * 4,
         scratch_shapes=[
+            pltpu.SMEM((1, 8), jnp.int32),
+            pltpu.VMEM((1, HD), F32),
+            pltpu.VMEM((1, HD), F32),
+            pltpu.VMEM((2, HD), F32),
             pltpu.VMEM((T, HK * HD), BF),
             pltpu.VMEM((T, HK * HD), BF),
             pltpu.VMEM((2, 2, T, 1024), BF),
@@ -558,7 +569,6 @@
             pltpu.VMEM((2, 2, 2, T, HD), F32),
             pltpu.VMEM((2, 2, 2, T, HD), F32),
             pltpu.VMEM((2, 2, T, 1024), BF),
-            pltpu.VMEM((HD, HD), F32),
             pltpu.VMEM((8, HD), F32),
             pltpu.VMEM((2, 2, 2, T, HD), BF),
             pltpu.VMEM((2, 2, 2, T, HD), BF),
@@ -568,18 +578,18 @@
             pltpu.VMEM((2, 2, T, HD), BF),
             pltpu.VMEM((T, HK * HD), BF),
             pltpu.VMEM((T, HK * HD), BF),
-            pltpu.VMEM((16, 2, 8, HD), F32),
-            pltpu.VMEM((16, 2, 8, HD), F32),
-            dma((6,)),
+            pltpu.VMEM((16, 1, HD), F32),
+            pltpu.VMEM((16, 1, HD), F32),
+            dma((9,)),
         ]
         + [s for s in sends for _ in range(2)]
         + [dma((2,)), dma((2,)), dma((2,))]
         + [dma((16,)) for _ in range(4)]
-        + [dma((2,))],
+        + [dma((3,))],
         compiler_params=pltpu.CompilerParams(
-            collective_id=0, has_side_effects=True, vmem_limit_bytes=60 * 1024 * 1024
+            collective_id=0, has_side_effects=True, vmem_limit_bytes=44 * 1024 * 1024
         ),
-    )(block_order, queries, keys, values, q_gain.reshape(1, HD), k_gain.reshape(1, HD), out_grad)
+    )(*(pltpu.with_memory_space_constraint(x, pltpu.HBM) for x in operands))
     return pl.pallas_call(
         settle,
         out_shape=(
@@ -591,15 +601,8 @@
         ),
         in_specs=[hbm] * 4,
         out_specs=(hbm,) * 5,
-        scratch_shapes=[
-            pltpu.VMEM((1, T, 32 * HD), BF),
-            pltpu.VMEM((1, T, HK * HD), BF),
-            pltpu.VMEM((1, T, HK * HD), BF),
-            pltpu.VMEM((2, HD), F32),
-            dma((7,)),
-            dma((8,)),
-        ],
-        compiler_params=pltpu.CompilerParams(vmem_limit_bytes=60 * 1024 * 1024),
+        scratch_shapes=[dma((8,))],
+        compiler_params=pltpu.CompilerParams(vmem_limit_bytes=16 * 1024 * 1024),
     )(*results)
 
 

time: 63.4 us -> 55.8 us (0.88)
  Pallas kernels: 62.7 us -> 55 us
    pallas_call x1, Pallas kernels: 60.5 us -> 53.9 us  [on_device(): pl.pallas_call(kernel, out_shape=(jax.ShapeDtypeStruct(queries.shape, BF)...]
    pallas_call x1, Pallas kernels: 2.18 us -> 1.13 us  [on_device(): pl.pallas_call(settle, out_shape=(jax.ShapeDtypeStruct(queries.shape, BF)...]
where the time goes in v2:
time: 55.8 us; the launch traced here: 55.7 us
  Pallas kernels  55 us (99%)
  between operations  0.64 us (1%)
    pallas_call x1, Pallas kernels, on_device(): pl.pallas_call(kernel, out_shape=(jax.ShapeDtypeStruct(queries.shape, BF)...  53.9 us
    pallas_call x1, Pallas kernels, on_device(): pl.pallas_call(settle, out_shape=(jax.ShapeDtypeStruct(queries.shape, BF)...  1.13 us

profile of v2, /device:TPU:1, one launch (start us, length us, event | category | flops | bytes accessed | tf_op | source)
XLA Modules:
  0.0 55.7 jit_solution(17431959833543544550)
XLA Ops:
  0.6 53.9 %shard_map.110 = (bf16[1,128,4096]{2,1,0:T(8,128)(2,1)S(1)}, bf16[1,128,512]{2,1,0:T(8,128)(2,1)S(1)}, bf16[1,128,512]{2,1,0:T(8,128)(2,1)S(1)}, f32[2,128]{1,0:T(2,128)S(1)}) custom-call(s32[1,8]{1,0:T(1,128)} %order_hbm.1, bf16[1,128,4096]{2,1,0:T(8,128)(2,1)} %q_hbm.1, bf16[1,128,512]{2,1,0:T(8,128)(2,1)} %k_hbm.1, bf16[1,128,512]{2,1,0:T(8,128)(2,1)} %v_hbm.1, ...), custom_call_target="tpu_custom_call" | custom-call | tf_op jit(solution)/shard_map/pallas_call | solution.py:537
  54.6 1.1 %shard_map.111 = (bf16[1,128,4096]{2,1,0:T(8,128)(2,1)}, bf16[1,128,512]{2,1,0:T(8,128)(2,1)}, bf16[1,128,512]{2,1,0:T(8,128)(2,1)}, f32[128]{0:T(128)}, f32[128]{0:T(128)}) custom-call(bf16[1,128,4096]{2,1,0:T(8,128)(2,1)S(1)} %get-tuple-element.9.dq, bf16[1,128,512]{2,1,0:T(8,128)(2,1)S(1)} %get-tuple-element.10.dk, ...), custom_call_target="tpu_custom_call" | custom-call | tf_op jit(solution)/shard_map/pallas_call | solution.py:593

commit v3 on v2

--- a/solution.py
+++ b/solution.py
@@ -1,4 +1,3 @@
-import functools
 import math
 
 import jax
@@ -23,8 +22,8 @@
 NT = (((1,), (1,)), ((), ()))
 NN = (((1,), (0,)), ((), ()))
 
-STEPS_FORWARD = (4, 7)
-STEPS_REDUCE = (4, 7)
+NEAR_SLOTS = (0, 1, 3)
+FAR_SLOTS = (2,)
 
 
 def dot(a, b, dims):
@@ -55,15 +54,16 @@
     g_cols[u, :, out] = jnp.concatenate([g2[:, :HD].T, g2[:, HD:].T], 1).astype(BF)
 
 
-def softmax_part(u, r, kv, q_normed, g_cols, bias, e_all, x_all, stat, w_all):
+def softmax_part(u, r, slots, kv, q_normed, g_cols, bias, e_all, x_all, sums, stat, w_all):
     rel = r // 4
     cols = pl.ds(pl.multiple_of(r * 256, 256), 256)
     qn = q_normed[u, :, cols]
     g = g_cols[u, :, cols]
-    total = jnp.zeros((8, 256), F32)
-    cross = jnp.zeros((8, 256), F32)
+    first = slots == NEAR_SLOTS
+    total = jnp.zeros((8, 256), F32) if first else sums[0, :, cols]
+    cross = jnp.zeros((8, 256), F32) if first else sums[1, :, cols]
     half = T // 2
-    for j in range(0, 8, 2):
+    for j in (2 * slot for slot in slots):
         s = dot(kv[u, 0, j : j + 2].reshape(2 * T, HD), qn, NN)
         d = dot(kv[u, 1, j : j + 2].reshape(2 * T, HD), g, NN)
         for b in range(4):
@@ -76,6 +76,10 @@
             cross = cross + jnp.sum(x.reshape(half // 8, 8, 256), 0)
             e_all[u, row : row + half, cols] = e.astype(BF)
             x_all[u, row : row + half, cols] = x.astype(BF)
+    if first:
+        sums[0, :, cols] = total
+        sums[1, :, cols] = cross
+        return
     inv = 1.0 / jnp.sum(total, 0, keepdims=True)
     row_dots = jnp.sum(cross, 0, keepdims=True) * inv
     stat[u, 0, :, cols] = jnp.broadcast_to(inv * SCALE, (8, 256))
@@ -94,18 +98,17 @@
 
 
 def query_part(u, r, kt, e_all, x_all, stat, q_unit, q_factor, gain_cols, dq_buf):
-    rel = r // 2
-    rows = pl.ds(pl.multiple_of(r * 512, 512), 512)
+    rel = r
+    rows = pl.ds(pl.multiple_of(r * 1024, 1024), 1024)
     x = dot(kt[u], x_all[u, :, rows], NN)
     e = dot(kt[u], e_all[u, :, rows], NN)
     dq = (x - e * stat[u, 1, 0:1, rows]) * stat[u, 0, 0:1, rows]
     unit = q_unit[u, :, rows]
     gain = gain_cols[...]
-    scaled = dq * jnp.concatenate([gain, gain], 1)
+    scaled = dq * jnp.concatenate([gain] * 4, 1)
     mean = jnp.mean(scaled * unit, 0, keepdims=True)
     out = q_factor[u, 0:1, rows] * (scaled - unit * mean)
-    cols = pl.ds(pl.multiple_of((r % 2) * 512, 512), 512)
-    dq_buf[u, rel, :, cols] = jnp.concatenate([out[:, i * HD : i * HD + HD].T for i in range(4)], 1).astype(BF)
+    dq_buf[u, rel] = jnp.concatenate([out[:, i * HD : i * HD + HD].T for i in range(8)], 1).astype(BF)
 
 
 def kernel(
@@ -139,6 +142,7 @@
     bias,
     e_all,
     x_all,
+    sums,
     stat,
     w_all,
     near_sum,
@@ -151,6 +155,9 @@
     b2_in,
     sib_out,
     sib_in,
+    fin_sum,
+    fin_factor,
+    fin_unit,
     dk_buf,
     dv_buf,
     ga_in,
@@ -206,12 +213,21 @@
 
     barrier = pltpu.get_barrier_semaphore()
 
-    def greet(r, carry):
-        pl.semaphore_signal(barrier, inc=1, device_id=ring_peer(lax.rem(ring_at + r, 16)), device_id_type=MESH)
-        pl.semaphore_signal(barrier, inc=1, device_id=plane_peer(lax.rem(dp_xy + r, 16)), device_id_type=MESH)
+    def greet(dev):
+        pl.semaphore_signal(barrier, inc=1, device_id=dev, device_id_type=MESH)
+
+    def greet_ring(i, carry):
+        greet({"dp": dp_xy * 2 + 1 - dp_z, "ctx": i})
         return carry
 
-    lax.fori_loop(1, 16, greet, 0)
+    def greet_plane(r, carry):
+        greet(plane_peer(lax.rem(dp_xy + r, 16)))
+        return carry
+
+    for i in (near[0], near[1], lax.rem(chip + 2, 4)):
+        for k in range(2):
+            greet({"ctx": 2 * i + k})
+    greet({"ctx": sibling})
     loads = [
         pltpu.make_async_copy(k_hbm.at[0], k_in, load_sem.at[0]),
         pltpu.make_async_copy(k_gain_hbm, k_gain, load_sem.at[6]),
@@ -221,6 +237,8 @@
     ]
     for c in loads:
         c.start()
+    lax.fori_loop(0, 8, greet_ring, 0)
+    lax.fori_loop(1, 16, greet_plane, 0)
     load_q = []
     for u in range(2):
         pair = (
@@ -300,15 +318,16 @@
             stage1_arrival(u, d, src_core, d).wait_recv()
             stage2(u, d, src_core).start()
 
-    def finish_gather(u):
+    def near_gather(u):
         for src_core in range(2):
             for d in range(2):
                 stage1_arrival(u, d, src_core, 1 - d).wait_recv()
         sibling_kv_arrival(u).wait_recv()
+
+    def far_gather(u):
         for src_core in range(2):
             for d in range(2):
                 stage2_arrival(u, d, src_core).wait_recv()
-        kt[u] = kv[u, 0].reshape(KEYS, HD).T
 
     def prepare_rows(u, rel):
         if rel == 0:
@@ -346,27 +365,34 @@
         return remote(sib_out.at[u], sib_in.at[u], sb_send.at[u], sb_recv.at[u], {"ctx": sibling})
 
     def key_sums(u, slot):
-        sums = key_part(u, slot, e_all, x_all, w_all)
+        both = key_part(u, slot, e_all, x_all, w_all)
         k_rows = kv[u, 0, 2 * slot : 2 * slot + 2].reshape(2 * T, HD).astype(F32)
-        gain_acc[...] += jnp.sum((sums[0] * k_rows).reshape(32, 8, HD), 0)
-        return sums
-
-    def reduce_start(u):
-        sums = key_sums(u, 2)
+        gain_acc[...] += jnp.sum((both[0] * k_rows).reshape(32, 8, HD), 0)
+        return [x.reshape(2, T, HD) for x in both]
+
+    def far_sums(u):
+        both = key_sums(u, 2)
         for d in range(2):
-            b1_out[u, d] = sums[d].reshape(2, T, HD).astype(BF)
+            b1_out[u, d] = both[d].astype(BF)
+
+    def far_start(u):
         for kk in range(2):
             for d in range(2):
                 b1(u, d, kk).start()
-        for d, slot in ((0, 1), (1, 3)):
-            sums = key_sums(u, slot)
-            for dest_core in range(2):
-                b2_out[u, d, dest_core, 1 - d] = sums[1 - d][dest_core * T : dest_core * T + T].astype(BF)
-                b2(u, d, dest_core, 1 - d).start()
-            near_sum[u, d] = sums[d].reshape(2, T, HD)
-        sums = key_sums(u, 0)
+
+    def near_sums(u, d):
+        both = key_sums(u, (1, 3)[d])
+        b2_out[u, d, :, 1 - d] = both[1 - d].astype(BF)
+        near_sum[u, d] = both[d]
+
+    def near_start(u, d):
+        for dest_core in range(2):
+            b2(u, d, dest_core, 1 - d).start()
+
+    def own_sums(u):
+        both = key_sums(u, 0)
         for part in range(2):
-            own_sum[u, part] = sums[part].reshape(2, T, HD)
+            own_sum[u, part] = both[part]
             sib_out[u, part] = own_sum[u, part, other].astype(BF)
         sibling_sum(u).start()
 
@@ -376,26 +402,33 @@
             b2_out[u, d, kk, d] = (near_sum[u, d, kk] + b1_in[u, d, kk].astype(F32)).astype(BF)
             b2(u, d, kk, d).start()
 
-    def reduce_finish(u):
+    def early_finish(u):
         sibling_sum(u).wait_recv()
         for d in range(2):
             for src_core in range(2):
-                for part in range(2):
-                    b2_arrival(u, d, src_core, part).wait_recv()
+                b2_arrival(u, d, src_core, 1 - d).wait_recv()
         for rel in range(2):
             at = core if rel == 0 else other
-            sums = []
             for part in range(2):
                 own = own_sum[u, part, core] if rel == 0 else sib_in[u, part].astype(F32)
-                sums.append(own + b2_in[u, 0, at, part].astype(F32) + b2_in[u, 1, at, part].astype(F32))
+                fin_sum[rel, part] = own + b2_in[u, 1 - part, at, part].astype(F32)
+            block = k_in[:, pl.ds(pl.multiple_of(at * 256 + u * HD, HD), HD)].astype(F32)
+            factor = lax.rsqrt(jnp.mean(block * block, -1, keepdims=True) + EPS)
+            fin_factor[rel] = jnp.broadcast_to(factor, (T, HD))
+            fin_unit[rel] = block * factor
+
+    def late_finish(u):
+        for d in range(2):
+            for src_core in range(2):
+                b2_arrival(u, d, src_core, d).wait_recv()
+        for rel in range(2):
+            at = core if rel == 0 else other
             cols = pl.ds(pl.multiple_of(at * 256 + u * HD, HD), HD)
-            block = k_in[:, cols].astype(F32)
-            factor = lax.rsqrt(jnp.mean(block * block, -1, keepdims=True) + EPS)
-            unit = block * factor
-            scaled = sums[0] * k_gain_row
+            unit = fin_unit[rel]
+            scaled = (fin_sum[rel, 0] + b2_in[u, 0, at, 0].astype(F32)) * k_gain_row
             mean = jnp.mean(scaled * unit, -1, keepdims=True)
-            dk_buf[:, cols] = (factor * (scaled - unit * mean)).astype(BF)
-            dv_buf[:, cols] = sums[1].astype(BF)
+            dk_buf[:, cols] = (fin_factor[rel] * (scaled - unit * mean)).astype(BF)
+            dv_buf[:, cols] = (fin_sum[rel, 1] + b2_in[u, 1, at, 1].astype(F32)).astype(BF)
 
     def out_local(u):
         return pltpu.make_async_copy(dq_buf.at[u, 0], dq_hbm.at[0, :, head_cols(core, u)], out_sem.at[u])
@@ -406,22 +439,23 @@
     def out_arrival(u):
         return remote(dq_buf.at[u, 1], dq_hbm.at[0, :, head_cols(other, u)], ox_send.at[u], ox_recv.at[u], {"ctx": sibling})
 
-    def softmax_parts(u, hooks):
+    def softmax_parts(u, slots):
         def one(r, carry):
-            for at, hook in hooks.items():
-                pl.when(r == at)(hook)
-
-            softmax_part(u, r, kv, q_normed, g_cols, bias, e_all, x_all, stat, w_all)
+            softmax_part(u, r, slots, kv, q_normed, g_cols, bias, e_all, x_all, sums, stat, w_all)
             return carry
 
         lax.fori_loop(0, 8, one, 0)
 
-    def query_parts(u, lo, hi):
+    def query_parts(u):
+        kt[u] = kv[u, 0].reshape(KEYS, HD).T
+
         def one(r, carry):
             query_part(u, r, kt, e_all, x_all, stat, q_unit, q_factor, gain_cols, dq_buf)
             return carry
 
-        lax.fori_loop(lo, hi, one, 0)
+        lax.fori_loop(0, 2, one, 0)
+        out_local(u).start()
+        out_remote(u).start()
 
     gather_start(0)
     share(0)
@@ -437,18 +471,35 @@
     for at in by_core:
         forward(0, at)
     gather_start(1)
+    prepare_rows(0, 1)
     prepare_rows(1, 0)
-    prepare_rows(0, 1)
     prepare_rows(1, 1)
-    finish_gather(0)
-    softmax_parts(0, {at: functools.partial(forward, 1, k) for at, k in zip(STEPS_FORWARD, by_core)})
-    reduce_start(0)
-    query_parts(0, 0, 4)
-    out_local(0).start()
-    out_remote(0).start()
-    finish_gather(1)
-    softmax_parts(1, {at: functools.partial(reduce_middle, 0, k) for at, k in zip(STEPS_REDUCE, range(2))})
-    reduce_start(1)
+    near_gather(0)
+    softmax_parts(0, NEAR_SLOTS)
+    far_gather(0)
+    softmax_parts(0, FAR_SLOTS)
+    far_sums(0)
+    forward(1, core)
+    near_sums(0, 0)
+    near_sums(0, 1)
+    forward(1, other)
+    far_start(0)
+    near_start(0, 0)
+    near_start(0, 1)
+    own_sums(0)
+    near_gather(1)
+    softmax_parts(1, NEAR_SLOTS)
+    far_gather(1)
+    softmax_parts(1, FAR_SLOTS)
+    reduce_middle(0, 0)
+    far_sums(1)
+    far_start(1)
+    near_sums(1, 0)
+    near_start(1, 0)
+    reduce_middle(0, 1)
+    near_sums(1, 1)
+    near_start(1, 1)
+    own_sums(1)
 
     def ga(r):
         return remote(ga_in.at[ring_at], ga_in.at[ring_at], ga_send.at[r], ga_recv.at[ring_at], ring_peer(lax.rem(ring_at + r, 16)))
@@ -473,36 +524,26 @@
 
     gb_in[dp_xy] = jnp.sum(gain_acc[...], 0, keepdims=True)
     for_peers(lambda r: gb(r).start())
-    query_parts(1, 0, 4)
-    out_local(1).start()
-    out_remote(1).start()
+    query_parts(0)
+    query_parts(1)
     for_peers(lambda r: gb_arrival(r).wait_recv())
     ga_in[ring_at] = jnp.sum(gb_in[...], 0)
     for_peers(lambda r: ga(r).start())
     for kk in range(2):
         reduce_middle(1, kk)
-    reduce_finish(0)
-    reduce_finish(1)
-    fin_k = pltpu.make_async_copy(dk_buf, dk_hbm.at[0], fin_sem.at[0])
-    fin_v = pltpu.make_async_copy(dv_buf, dv_hbm.at[0], fin_sem.at[1])
-    fin_k.start()
-    fin_v.start()
-    for_peers(lambda r: ga_arrival(r).wait_recv())
-    gain_sum = jnp.sum(ga_in[...], 0)
-    gains_out[0:1] = gain_sum / q_gain[...]
-    gains_out[1:2] = gain_sum / k_gain_row
-    fin_g = pltpu.make_async_copy(gains_out, gains_hbm, fin_sem.at[2])
-    fin_g.start()
-
+    early_finish(0)
+    late_finish(0)
+    early_finish(1)
     for u in range(2):
         for d in range(2):
             for dest_core in range(2):
                 for part in range(2):
                     stage1(u, d, dest_core, part).wait_send()
-                    b2(u, d, dest_core, part).wait_send()
                 stage2(u, d, dest_core).wait_send()
-            for kk in range(2):
-                b1(u, d, kk).wait_send()
+                b1(u, d, dest_core).wait_send()
+                b2(u, d, dest_core, 1 - d).wait_send()
+                if u == 0:
+                    b2(u, d, dest_core, d).wait_send()
         sibling_kv(u).wait_send()
         sibling_sum(u).wait_send()
         for c in q_exchange(u):
@@ -510,11 +551,25 @@
         out_local(u).wait()
         out_remote(u).wait_send()
         out_arrival(u).wait_recv()
+    for_peers(lambda r: gb(r).wait_send())
     for_peers(lambda r: ga(r).wait_send())
-    for_peers(lambda r: gb(r).wait_send())
+    for_peers(lambda r: ga_arrival(r).wait_recv())
+    gain_sum = jnp.sum(ga_in[...], 0)
+    gains_out[0:1] = gain_sum / q_gain[...]
+    gains_out[1:2] = gain_sum / k_gain_row
+    fin_g = pltpu.make_async_copy(gains_out, gains_hbm, fin_sem.at[2])
+    fin_g.start()
+    late_finish(1)
+    fin_k = pltpu.make_async_copy(dk_buf, dk_hbm.at[0], fin_sem.at[0])
+    fin_v = pltpu.make_async_copy(dv_buf, dv_hbm.at[0], fin_sem.at[1])
+    fin_k.start()
+    fin_v.start()
+    for d in range(2):
+        for dest_core in range(2):
+            b2(1, d, dest_core, d).wait_send()
+    fin_g.wait()
     fin_k.wait()
     fin_v.wait()
-    fin_g.wait()
 
 
 def settle(dq, dk, dv, gains, dq_out, dk_out, dv_out, q_gain_out, k_gain_out, sems):
@@ -564,6 +619,7 @@
             pltpu.VMEM((2, 8, T, T), F32),
             pltpu.VMEM((2, KEYS, ROWS), BF),
             pltpu.VMEM((2, KEYS, ROWS), BF),
+            pltpu.VMEM((2, 8, ROWS), F32),
             pltpu.VMEM((2, 2, 8, ROWS), F32),
             pltpu.VMEM((2, 3 * HD, ROWS), BF),
             pltpu.VMEM((2, 2, 2, T, HD), F32),
@@ -576,6 +632,9 @@
             pltpu.VMEM((2, 2, 2, 2, T, HD), BF),
             pltpu.VMEM((2, 2, T, HD), BF),
             pltpu.VMEM((2, 2, T, HD), BF),
+            pltpu.VMEM((2, 2, T, HD), F32),
+            pltpu.VMEM((2, T, HD), F32),
+            pltpu.VMEM((2, T, HD), F32),
             pltpu.VMEM((T, HK * HD), BF),
             pltpu.VMEM((T, HK * HD), BF),
             pltpu.VMEM((16, 1, HD), F32),

time: 55.8 us -> 54.4 us (0.975)
  Pallas kernels: 55 us -> 53.7 us
    pallas_call x1, Pallas kernels: 53.9 us -> 52.6 us  [on_device(): pl.pallas_call(kernel, out_shape=(jax.ShapeDtypeStruct(queries.shape, BF)...]
where the time goes in v3:
time: 54.4 us; the launch traced here: 54.3 us
  Pallas kernels  53.7 us (99%)
  between operations  0.64 us (1%)
    pallas_call x1, Pallas kernels, on_device(): pl.pallas_call(kernel, out_shape=(jax.ShapeDtypeStruct(queries.shape, BF)...  52.6 us
    pallas_call x1, Pallas kernels, on_device(): pl.pallas_call(settle, out_shape=(jax.ShapeDtypeStruct(queries.shape, BF)...  1.13 us

profile of v3, /device:TPU:1, one launch (start us, length us, event | category | flops | bytes accessed | tf_op | source)
XLA Modules:
  0.0 54.3 jit_solution(537091401286410811)
XLA Ops:
  0.6 52.6 %shard_map.110 = (bf16[1,128,4096]{2,1,0:T(8,128)(2,1)S(1)}, bf16[1,128,512]{2,1,0:T(8,128)(2,1)S(1)}, bf16[1,128,512]{2,1,0:T(8,128)(2,1)S(1)}, f32[2,128]{1,0:T(2,128)S(1)}) custom-call(s32[1,8]{1,0:T(1,128)} %order_hbm.1, bf16[1,128,4096]{2,1,0:T(8,128)(2,1)} %q_hbm.1, bf16[1,128,512]{2,1,0:T(8,128)(2,1)} %k_hbm.1, bf16[1,128,512]{2,1,0:T(8,128)(2,1)} %v_hbm.1, ...), custom_call_target="tpu_custom_call" | custom-call | tf_op jit(solution)/shard_map/pallas_call | solution.py:592
  53.2 1.1 %shard_map.111 = (bf16[1,128,4096]{2,1,0:T(8,128)(2,1)}, bf16[1,128,512]{2,1,0:T(8,128)(2,1)}, bf16[1,128,512]{2,1,0:T(8,128)(2,1)}, f32[128]{0:T(128)}, f32[128]{0:T(128)}) custom-call(bf16[1,128,4096]{2,1,0:T(8,128)(2,1)S(1)} %get-tuple-element.9.dq, bf16[1,128,512]{2,1,0:T(8,128)(2,1)S(1)} %get-tuple-element.10.dk, ...), custom_call_target="tpu_custom_call" | custom-call | tf_op jit(solution)/shard_map/pallas_call | solution.py:652

commit v4 on v3

--- a/solution.py
+++ b/solution.py
@@ -55,13 +55,13 @@
 
 
 def softmax_part(u, r, slots, kv, q_normed, g_cols, bias, e_all, x_all, sums, stat, w_all):
-    rel = r // 4
-    cols = pl.ds(pl.multiple_of(r * 256, 256), 256)
+    rel = r // 2
+    cols = pl.ds(pl.multiple_of(r * 512, 512), 512)
     qn = q_normed[u, :, cols]
     g = g_cols[u, :, cols]
     first = slots == NEAR_SLOTS
-    total = jnp.zeros((8, 256), F32) if first else sums[0, :, cols]
-    cross = jnp.zeros((8, 256), F32) if first else sums[1, :, cols]
+    total = jnp.zeros((8, 512), F32) if first else sums[0, :, cols]
+    cross = jnp.zeros((8, 512), F32) if first else sums[1, :, cols]
     half = T // 2
     for j in (2 * slot for slot in slots):
         s = dot(kv[u, 0, j : j + 2].reshape(2 * T, HD), qn, NN)
@@ -69,11 +69,11 @@
         for b in range(4):
             at, row = b * half, j * T + b * half
             tile = bias[rel, j + b // 2, (b % 2) * half : (b % 2 + 1) * half, :]
-            tile = jnp.concatenate([tile, tile], 1)
+            tile = jnp.concatenate([tile] * 4, 1)
             e = jnp.exp2(s[at : at + half] * EXP2_SCALE + tile)
             x = e * d[at : at + half]
-            total = total + jnp.sum(e.reshape(half // 8, 8, 256), 0)
-            cross = cross + jnp.sum(x.reshape(half // 8, 8, 256), 0)
+            total = total + jnp.sum(e.reshape(half // 8, 8, 512), 0)
+            cross = cross + jnp.sum(x.reshape(half // 8, 8, 512), 0)
             e_all[u, row : row + half, cols] = e.astype(BF)
             x_all[u, row : row + half, cols] = x.astype(BF)
     if first:
@@ -82,8 +82,8 @@
         return
     inv = 1.0 / jnp.sum(total, 0, keepdims=True)
     row_dots = jnp.sum(cross, 0, keepdims=True) * inv
-    stat[u, 0, :, cols] = jnp.broadcast_to(inv * SCALE, (8, 256))
-    stat[u, 1, :, cols] = jnp.broadcast_to(row_dots, (8, 256))
+    stat[u, 0, :, cols] = jnp.broadcast_to(inv * SCALE, (8, 512))
+    stat[u, 1, :, cols] = jnp.broadcast_to(row_dots, (8, 512))
     scaled = qn.astype(F32) * inv
     w_all[u, 0:128, cols] = (g.astype(F32) * inv).astype(BF)
     w_all[u, 128:256, cols] = (scaled * -row_dots).astype(BF)
@@ -444,7 +444,7 @@
             softmax_part(u, r, slots, kv, q_normed, g_cols, bias, e_all, x_all, sums, stat, w_all)
             return carry
 
-        lax.fori_loop(0, 8, one, 0)
+        lax.fori_loop(0, 4, one, 0, unroll=2)
 
     def query_parts(u):
         kt[u] = kv[u, 0].reshape(KEYS, HD).T
@@ -525,12 +525,12 @@
     gb_in[dp_xy] = jnp.sum(gain_acc[...], 0, keepdims=True)
     for_peers(lambda r: gb(r).start())
     query_parts(0)
-    query_parts(1)
     for_peers(lambda r: gb_arrival(r).wait_recv())
     ga_in[ring_at] = jnp.sum(gb_in[...], 0)
     for_peers(lambda r: ga(r).start())
-    for kk in range(2):
-        reduce_middle(1, kk)
+    reduce_middle(1, 0)
+    reduce_middle(1, 1)
+    query_parts(1)
     early_finish(0)
     late_finish(0)
     early_finish(1)

time: 54.4 us -> 54.6 us (level)
  no operation moved by 1% of the time
where the time goes in v4:
time: 54.6 us; the launch traced here: 54.5 us
  Pallas kernels  53.9 us (99%)
  between operations  0.64 us (1%)
    pallas_call x1, Pallas kernels, on_device(): pl.pallas_call(kernel, out_shape=(jax.ShapeDtypeStruct(queries.shape, BF)...  52.7 us
    pallas_call x1, Pallas kernels, on_device(): pl.pallas_call(settle, out_shape=(jax.ShapeDtypeStruct(queries.shape, BF)...  1.13 us

profile of v4, /device:TPU:1, one launch (start us, length us, event | category | flops | bytes accessed | tf_op | source)
XLA Modules:
  0.0 54.5 jit_solution(966403378591470468)
XLA Ops:
  0.6 52.7 %shard_map.110 = (bf16[1,128,4096]{2,1,0:T(8,128)(2,1)S(1)}, bf16[1,128,512]{2,1,0:T(8,128)(2,1)S(1)}, bf16[1,128,512]{2,1,0:T(8,128)(2,1)S(1)}, f32[2,128]{1,0:T(2,128)S(1)}) custom-call(s32[1,8]{1,0:T(1,128)} %order_hbm.1, bf16[1,128,4096]{2,1,0:T(8,128)(2,1)} %q_hbm.1, bf16[1,128,512]{2,1,0:T(8,128)(2,1)} %k_hbm.1, bf16[1,128,512]{2,1,0:T(8,128)(2,1)} %v_hbm.1, ...), custom_call_target="tpu_custom_call" | custom-call | tf_op jit(solution)/shard_map/pallas_call | solution.py:592
  53.4 1.1 %shard_map.111 = (bf16[1,128,4096]{2,1,0:T(8,128)(2,1)}, bf16[1,128,512]{2,1,0:T(8,128)(2,1)}, bf16[1,128,512]{2,1,0:T(8,128)(2,1)}, f32[128]{0:T(128)}, f32[128]{0:T(128)}) custom-call(bf16[1,128,4096]{2,1,0:T(8,128)(2,1)S(1)} %get-tuple-element.9.dq, bf16[1,128,512]{2,1,0:T(8,128)(2,1)S(1)} %get-tuple-element.10.dk, ...), custom_call_target="tpu_custom_call" | custom-call | tf_op jit(solution)/shard_map/pallas_call | solution.py:652

commit v5 on v4

--- a/solution.py
+++ b/solution.py
@@ -525,12 +525,12 @@
     gb_in[dp_xy] = jnp.sum(gain_acc[...], 0, keepdims=True)
     for_peers(lambda r: gb(r).start())
     query_parts(0)
+    query_parts(1)
     for_peers(lambda r: gb_arrival(r).wait_recv())
     ga_in[ring_at] = jnp.sum(gb_in[...], 0)
     for_peers(lambda r: ga(r).start())
     reduce_middle(1, 0)
     reduce_middle(1, 1)
-    query_parts(1)
     early_finish(0)
     late_finish(0)
     early_finish(1)

time: 54.6 us -> 54.6 us (level)
  no operation moved by 1% of the time
where the time goes in v5:
time: 54.6 us; the launch traced here: 54.5 us
  Pallas kernels  53.9 us (99%)
  between operations  0.64 us (1%)
    pallas_call x1, Pallas kernels, on_device(): pl.pallas_call(kernel, out_shape=(jax.ShapeDtypeStruct(queries.shape, BF)...  52.7 us
    pallas_call x1, Pallas kernels, on_device(): pl.pallas_call(settle, out_shape=(jax.ShapeDtypeStruct(queries.shape, BF)...  1.13 us

profile of v5, /device:TPU:1, one launch (start us, length us, event | category | flops | bytes accessed | tf_op | source)
XLA Modules:
  0.0 54.5 jit_solution(6304294803712756975)
XLA Ops:
  0.6 52.7 %shard_map.110 = (bf16[1,128,4096]{2,1,0:T(8,128)(2,1)S(1)}, bf16[1,128,512]{2,1,0:T(8,128)(2,1)S(1)}, bf16[1,128,512]{2,1,0:T(8,128)(2,1)S(1)}, f32[2,128]{1,0:T(2,128)S(1)}) custom-call(s32[1,8]{1,0:T(1,128)} %order_hbm.1, bf16[1,128,4096]{2,1,0:T(8,128)(2,1)} %q_hbm.1, bf16[1,128,512]{2,1,0:T(8,128)(2,1)} %k_hbm.1, bf16[1,128,512]{2,1,0:T(8,128)(2,1)} %v_hbm.1, ...), custom_call_target="tpu_custom_call" | custom-call | tf_op jit(solution)/shard_map/pallas_call | solution.py:592
  53.4 1.1 %shard_map.111 = (bf16[1,128,4096]{2,1,0:T(8,128)(2,1)}, bf16[1,128,512]{2,1,0:T(8,128)(2,1)}, bf16[1,128,512]{2,1,0:T(8,128)(2,1)}, f32[128]{0:T(128)}, f32[128]{0:T(128)}) custom-call(bf16[1,128,4096]{2,1,0:T(8,128)(2,1)S(1)} %get-tuple-element.9.dq, bf16[1,128,512]{2,1,0:T(8,128)(2,1)S(1)} %get-tuple-element.10.dk, ...), custom_call_target="tpu_custom_call" | custom-call | tf_op jit(solution)/shard_map/pallas_call | solution.py:652

commit v6 on v3

--- a/solution.py
+++ b/solution.py
@@ -417,18 +417,20 @@
             fin_factor[rel] = jnp.broadcast_to(factor, (T, HD))
             fin_unit[rel] = block * factor
 
-    def late_finish(u):
-        for d in range(2):
-            for src_core in range(2):
-                b2_arrival(u, d, src_core, d).wait_recv()
+    def late_finish(u, part):
+        for src_core in range(2):
+            b2_arrival(u, part, src_core, part).wait_recv()
         for rel in range(2):
             at = core if rel == 0 else other
             cols = pl.ds(pl.multiple_of(at * 256 + u * HD, HD), HD)
+            full = fin_sum[rel, part] + b2_in[u, part, at, part].astype(F32)
+            if part == 1:
+                dv_buf[:, cols] = full.astype(BF)
+                continue
             unit = fin_unit[rel]
-            scaled = (fin_sum[rel, 0] + b2_in[u, 0, at, 0].astype(F32)) * k_gain_row
+            scaled = full * k_gain_row
             mean = jnp.mean(scaled * unit, -1, keepdims=True)
             dk_buf[:, cols] = (fin_factor[rel] * (scaled - unit * mean)).astype(BF)
-            dv_buf[:, cols] = (fin_sum[rel, 1] + b2_in[u, 1, at, 1].astype(F32)).astype(BF)
 
     def out_local(u):
         return pltpu.make_async_copy(dq_buf.at[u, 0], dq_hbm.at[0, :, head_cols(core, u)], out_sem.at[u])
@@ -532,7 +534,8 @@
     for kk in range(2):
         reduce_middle(1, kk)
     early_finish(0)
-    late_finish(0)
+    late_finish(0, 1)
+    late_finish(0, 0)
     early_finish(1)
     for u in range(2):
         for d in range(2):
@@ -559,11 +562,12 @@
     gains_out[1:2] = gain_sum / k_gain_row
     fin_g = pltpu.make_async_copy(gains_out, gains_hbm, fin_sem.at[2])
     fin_g.start()
-    late_finish(1)
+    late_finish(1, 1)
+    fin_v = pltpu.make_async_copy(dv_buf, dv_hbm.at[0], fin_sem.at[1])
+    fin_v.start()
+    late_finish(1, 0)
     fin_k = pltpu.make_async_copy(dk_buf, dk_hbm.at[0], fin_sem.at[0])
-    fin_v = pltpu.make_async_copy(dv_buf, dv_hbm.at[0], fin_sem.at[1])
     fin_k.start()
-    fin_v.start()
     for d in range(2):
         for dest_core in range(2):
             b2(1, d, dest_core, d).wait_send()
@@ -573,10 +577,11 @@
 
 
 def settle(dq, dk, dv, gains, dq_out, dk_out, dv_out, q_gain_out, k_gain_out, sems):
-    pairs = [(gains.at[0], q_gain_out), (gains.at[1], k_gain_out), (dk, dk_out), (dv, dv_out)]
+    pairs = []
     for i in range(4):
         rows = pl.ds(i * 32, 32)
         pairs.append((dq.at[0, rows], dq_out.at[0, rows]))
+    pairs += [(dk, dk_out), (dv, dv_out), (gains.at[0], q_gain_out), (gains.at[1], k_gain_out)]
     copies = [pltpu.make_async_copy(a, b, sems.at[i]) for i, (a, b) in enumerate(pairs)]
     for c in copies:
         c.start()

time: 54.4 us -> 54.4 us (level)
  no operation moved by 1% of the time
where the time goes in v6:
time: 54.4 us; the launch traced here: 54.3 us
  Pallas kernels  53.7 us (99%)
  between operations  0.64 us (1%)
    pallas_call x1, Pallas kernels, on_device(): pl.pallas_call(kernel, out_shape=(jax.ShapeDtypeStruct(queries.shape, BF)...  52.6 us
    pallas_call x1, Pallas kernels, on_device(): pl.pallas_call(settle, out_shape=(jax.ShapeDtypeStruct(queries.shape, BF)...  1.12 us

profile of v6, /device:TPU:1, one launch (start us, length us, event | category | flops | bytes accessed | tf_op | source)
XLA Modules:
  0.0 54.3 jit_solution(4807595256241482329)
XLA Ops:
  0.6 52.6 %shard_map.110 = (bf16[1,128,4096]{2,1,0:T(8,128)(2,1)S(1)}, bf16[1,128,512]{2,1,0:T(8,128)(2,1)S(1)}, bf16[1,128,512]{2,1,0:T(8,128)(2,1)S(1)}, f32[2,128]{1,0:T(2,128)S(1)}) custom-call(s32[1,8]{1,0:T(1,128)} %order_hbm.1, bf16[1,128,4096]{2,1,0:T(8,128)(2,1)} %q_hbm.1, bf16[1,128,512]{2,1,0:T(8,128)(2,1)} %k_hbm.1, bf16[1,128,512]{2,1,0:T(8,128)(2,1)} %v_hbm.1, ...), custom_call_target="tpu_custom_call" | custom-call | tf_op jit(solution)/shard_map/pallas_call | solution.py:597
  53.2 1.1 %shard_map.111 = (bf16[1,128,4096]{2,1,0:T(8,128)(2,1)}, bf16[1,128,512]{2,1,0:T(8,128)(2,1)}, bf16[1,128,512]{2,1,0:T(8,128)(2,1)}, f32[128]{0:T(128)}, f32[128]{0:T(128)}) custom-call(bf16[1,128,4096]{2,1,0:T(8,128)(2,1)S(1)} %get-tuple-element.9.dq, bf16[1,128,512]{2,1,0:T(8,128)(2,1)S(1)} %get-tuple-element.10.dk, ...), custom_call_target="tpu_custom_call" | custom-call | tf_op jit(solution)/shard_map/pallas_call | solution.py:657
